TPU v7x, 32 devices: a whole 2x2x4 slice. The times are simulated.
32 devices in a mesh: ply: 2 (over x), tile: 16 (over z, y, core).
Axes of the slice: x: 2, y: 2, z: 4, core: 2. Of those that a mesh axis runs over, the one named last changes fastest.
Arguments:
- strain: float32 [4, 3, 16, 4096], P(None, None, None, 'tile'), may hold values from -6 to 6
- case_ids: int32 [4], replicated, may hold values from 0 to 3, each once
- angle_ids: int32 [48], P('ply'), may hold values from 0 to 3
- stiffening: float32 [48, 16, 4096], P('ply', None, 'tile'), may hold values from 0.5 to 8
- interface: float32 [48, 16, 4096], P('ply', None, 'tile'), may hold values from 0.5 to 4
Outputs:
- adjoint: float32 [4, 48, 16, 4096], P(None, 'ply', None, 'tile')
- through: float32 [48, 16, 4096], P('ply', None, 'tile')
Inputs may be any that keep to these rules, and one draw needn't show every extreme that they name: `case_ids`: each of the 4 load states is taken by exactly one load case.
All inputs are finite; a program needn't handle non-finite values.
Results may differ from a plain program's by a relative error of at most 0.0085.
Values sent between devices are 32-bit elements; how exact they have to be, the bound alone decides.
A program may use at most 64 MiB of HBM per device.

v0:
```python
import jax
import jax.numpy as jnp
from jax import lax
from jax.sharding import PartitionSpec as P

ITERS = 4


relaxation = 2.0 / 3.0
half_root = 0.7071067811865476
fibre_modulus = 1.0
trans_modulus = 0.5
shear_modulus = 0.3
linear_fibre = 0.3
linear_trans = 0.8
square_fibre = 0.5
square_trans = 1.0
square_shear = 0.8
cross_term = -0.35


def passed_along(array, axis, by):
    count = lax.axis_size(axis)
    pairs = [(i, i + by) for i in range(count) if 0 <= i + by < count]
    return lax.ppermute(array, axis, pairs)


def extended(block, sides, width):
    for axis, dim in sides:
        count = lax.axis_size(axis)
        forward = [(i, i + 1) for i in range(count - 1)]
        backward = [(target, source) for source, target in forward]
        low = lax.ppermute(
            lax.slice_in_dim(block, block.shape[dim] - width, None, axis=dim), axis, forward
        )
        high = lax.ppermute(lax.slice_in_dim(block, 0, width, axis=dim), axis, backward)
        block = jnp.concatenate([low, block, high], axis=dim)
    return block


def prefix_2(value, axis, join, neutral):
    count, mine = (lax.axis_size(axis), lax.axis_index(axis))
    pieces = lax.all_gather(value, axis)
    so_far = jnp.full_like(value, 0) + jnp.asarray(neutral, value.dtype)

    def hop(position, so_far):
        longer = join(so_far, pieces[position])
        return jnp.where(position < mine, longer, so_far)

    return lax.fori_loop(0, count - 1, hop, so_far)


def ply_tables(angles):
    one_hot = (angles[:, None] == jnp.arange(4, dtype=jnp.int32)[None, :]).astype(jnp.float32)
    ply_cosine = jnp.sum(
        one_hot * jnp.array([1.0, half_root, half_root, 0.0], jnp.float32)[None, :], axis=1
    )
    ply_sine = jnp.sum(
        one_hot * jnp.array([0.0, half_root, -half_root, 1.0], jnp.float32)[None, :], axis=1
    )
    ply_cosine = ply_cosine.reshape(-1, 1, 1)
    ply_sine = ply_sine.reshape(-1, 1, 1)
    cond_rows = 4.0 * ply_cosine * ply_cosine + ply_sine * ply_sine
    cond_cols = 4.0 * ply_sine * ply_sine + ply_cosine * ply_cosine
    cond_cross = 3.0 * ply_cosine * ply_sine
    return (cond_rows, cond_cols, cond_cross, ply_cosine, ply_sine)


def tsai_wu(strain_x, strain_y, strain_xy, ply_cosine, ply_sine):
    cos_sq = ply_cosine * ply_cosine
    sin_sq = ply_sine * ply_sine
    mixed = ply_cosine * ply_sine
    fibre_strain = cos_sq * strain_x + sin_sq * strain_y + mixed * strain_xy
    trans_strain = sin_sq * strain_x + cos_sq * strain_y - mixed * strain_xy
    shear_strain = 2.0 * mixed * (strain_y - strain_x) + (cos_sq - sin_sq) * strain_xy
    fibre_stress = fibre_modulus * fibre_strain
    trans_stress = trans_modulus * trans_strain
    shear_stress = shear_modulus * shear_strain
    first = linear_fibre + 2.0 * square_fibre * fibre_stress + 2.0 * cross_term * trans_stress
    second = linear_trans + 2.0 * square_trans * trans_stress + 2.0 * cross_term * fibre_stress
    return first + second + 2.0 * square_shear * shear_stress


def sweep(padded, source, stiffening, coupling_up, coupling_down, cond_rows, cond_cols, cond_cross):
    widths = [(0, 0)] * (padded.ndim - 2) + [(1, 1), (0, 0)]
    framed = jnp.pad(padded, widths)
    centre = framed[..., 1:-1, 1:-1, 1:-1]
    along_rows = framed[..., 1:-1, 2:, 1:-1] + framed[..., 1:-1, :-2, 1:-1]
    along_cols = framed[..., 1:-1, 1:-1, 2:] + framed[..., 1:-1, 1:-1, :-2]
    diagonal_pairs = (
        framed[..., 1:-1, 2:, 2:]
        + framed[..., 1:-1, :-2, :-2]
        - framed[..., 1:-1, 2:, :-2]
        - framed[..., 1:-1, :-2, 2:]
    )
    overhead = framed[..., 2:, 1:-1, 1:-1]
    beneath = framed[..., :-2, 1:-1, 1:-1]
    image = (
        cond_rows * (2.0 * centre - along_rows)
        + cond_cols * (2.0 * centre - along_cols)
        - 0.5 * cond_cross * diagonal_pairs
    )
    image = (
        image
        + coupling_up * (centre - overhead)
        + coupling_down * (centre - beneath)
        + stiffening * centre
    )
    diagonal_sum = 2.0 * cond_rows + 2.0 * cond_cols + coupling_up + coupling_down + stiffening
    return centre + relaxation * (source - image) / diagonal_sum


def combine_sum(earlier, later):
    return earlier + later


def body(strain, case_ids, angle_ids, stiffening, interface):
    ply_count = angle_ids.shape[0]
    chosen = jnp.take(strain, case_ids, axis=0)
    cond_rows, cond_cols, cond_cross, ply_cosine, ply_sine = ply_tables(angle_ids)
    source = tsai_wu(
        chosen[:, 0][:, None], chosen[:, 1][:, None], chosen[:, 2][:, None], ply_cosine, ply_sine
    )
    adjoint = jnp.zeros(source.shape, jnp.float32)
    lower_plane = passed_along(interface[-1:], "ply", 1)
    coupling_down = jnp.concatenate([lower_plane, interface[:-1]], axis=0)
    for iteration in range(ITERS):
        padded = extended(adjoint, (("ply", 1), ("tile", 3)), 1)
        adjoint = sweep(
            padded, source, stiffening, interface, coupling_down, cond_rows, cond_cols, cond_cross
        )
    summed = jnp.sum(adjoint * source, axis=0)
    running = jnp.cumsum(summed, axis=0)
    plane_total = running[-1]
    prefix = prefix_2(plane_total, "ply", combine_sum, jnp.zeros_like(plane_total))
    through = (running + prefix[None]) / (ply_count * lax.axis_size("ply"))
    return (adjoint, through)


def solution(mesh):
    return jax.shard_map(
        body,
        mesh=mesh,
        in_specs=(
            P(None, None, None, "tile"),
            P(),
            P("ply"),
            P("ply", None, "tile"),
            P("ply", None, "tile"),
        ),
        out_specs=(P(None, "ply", None, "tile"), P("ply", None, "tile")),
        check_vma=False,
    )
```

profile of v0, /device:TPU:5, one launch (start us, length us, event | category | flops | bytes accessed | tf_op | source)
XLA Modules:
  0.0 141.2 jit_solution(18410286680509812157)
XLA Ops:
  0.7 3.2 %collective-permute-start = (f32[4,1,16,256]{3,2,1,0:T(8,128)S(1)}, f32[4,1,16,256]{3,2,1,0:T(8,128)S(1)}, u32[]{:S(2)}, u32[]{:S(2)}) collective-permute-start(f32[4,1,16,256]{3,2,1,0:T(8,128)S(1)} %broadcast.119), channel_id=1, source_target_pairs={{0,16},{1,17},{2,18},{3,19},{4,20},{5,21},{6,22},{7,23},{8,24},{9,... | collective-permute-start | bytes 196616 | tf_op jit(solution)/shard_map/ppermute | solution.py:33
  3.9 1.3 collective-permute-start.1
  5.9 4.0 %collective-permute-start.4 = (f32[1,16,256]{2,1,0:T(8,128)S(1)}, f32[1,16,256]{2,1,0:T(8,128)S(1)}, u32[]{:S(2)}, u32[]{:S(2)}) collective-permute-start(f32[1,16,256]{2,1,0:T(8,128)S(1)} %slice.247), channel_id=1, source_target_pairs={{0,16},{1,17},{2,18},{3,19},{4,20},{5,21},{6,22},{7,23},{8,24},{9,... | collective-permute-start | bytes 49160 | tf_op jit(solution)/shard_map/ppermute | solution.py:25
  12.6 0.8 select_reduce_fusion
  14.3 1.5 %fusion.85 = (f32[4,26,16,1]{3,2,1,0:T(8,128)}, f32[4,26,16,1]{3,2,1,0:T(8,128)}) fusion(f32[4,26,16,256]{3,2,1,0:T(8,128)S(1)} %pad_maximum_fusion), kind=kLoop, calls=%fused_computation.179 | loop fusion | bytes 26624 | tf_op jit(solution)/shard_map/slice | solution.py:34
  15.8 1.7 %copy.72 = f32[4,26,16,1]{1,2,3,0:T(8,128)S(1)} copy(f32[4,26,16,1]{3,2,1,0:T(8,128)} %get-tuple-element.34) | data formatting | bytes 13312
  17.5 4.5 %collective-permute-start.2 = (f32[4,26,16,1]{1,2,3,0:T(8,128)S(1)}, f32[4,26,16,1]{1,2,3,0:T(8,128)S(1)}, u32[]{:S(2)}, u32[]{:S(2)}) collective-permute-start(f32[4,26,16,1]{1,2,3,0:T(8,128)S(1)} %copy.72), channel_id=1, source_target_pairs={{0,1},{1,2},{2,3},{3,4},{4,5},{5,6},{6,7},{7,8},{8,9},{9,10},{10,1... | collective-permute-start | bytes 19976 | tf_op jit(solution)/shard_map/ppermute | solution.py:33
  22.1 1.7 %copy.73 = f32[4,26,16,1]{1,2,3,0:T(8,128)S(1)} copy(f32[4,26,16,1]{3,2,1,0:T(8,128)} %get-tuple-element.35) | data formatting | bytes 13312
  23.8 1.9 %collective-permute-start.3 = (f32[4,26,16,1]{1,2,3,0:T(8,128)S(1)}, f32[4,26,16,1]{1,2,3,0:T(8,128)S(1)}, u32[]{:S(2)}, u32[]{:S(2)}) collective-permute-start(f32[4,26,16,1]{1,2,3,0:T(8,128)S(1)} %copy.73), channel_id=1, source_target_pairs={{1,0},{2,1},{3,2},{4,3},{5,4},{6,5},{7,6},{8,7},{9,8},{10,9},{11,1... | collective-permute-start | bytes 19976 | tf_op jit(solution)/shard_map/ppermute | solution.py:36
  25.7 1.1 pad_maximum_fusion.34
  27.3 2.5 %collective-permute-done.3 = f32[4,26,16,1]{1,2,3,0:T(8,128)S(1)} collective-permute-done((f32[4,26,16,1]{1,2,3,0:T(8,128)S(1)}, f32[4,26,16,1]{1,2,3,0:T(8,128)S(1)}, u32[]{:S(2)}, u32[]{:S(2)}) %collective-permute-start.3) | collective-permute-done | bytes 6688 | tf_op jit(solution)/shard_map/ppermute | solution.py:36
  29.9 1.4 copy.48
  31.4 3.6 %select_maximum_fusion.12 = f32[4,26,18,258]{3,2,1,0:T(8,128)S(1)} fusion(f32[4,26,16,1]{3,2,1,0:T(8,128)} %copy.48, f32[4,26,16,1]{3,2,1,0:T(8,128)S(1)} %copy.47, f32[4,1,16,256]{3,2,1,0:T(8,128)S(1)} %collective-permute-done.1, f32[4,24,16,256]{3,2,1,0:T(8,128)S(1)} %broadcast_in_dim.21, f32[4,1,16,256]{3,2,1,0:T(8,128)S(1)} %collective-permute-done), kind=kLoop, calls=%fused_computation.15 | loop fusion | flops 5795712 | bytes 3649152 | tf_op jit(solution)/shard_map/concatenate | solution.py:37
  35.1 5.9 %fusion.8 = f32[4,24,16,256]{3,2,1,0:T(8,128)S(1)} fusion(f32[4,24,16,256]{3,2,1,0:T(8,128)S(1)} %broadcast_in_dim.21, f32[4,1,16,256]{3,2,1,0:T(8,128)} %copy-done.38, f32[4,1,16,256]{3,2,1,0:T(8,128)} %copy-done.37, f32[4,26,18,258]{3,2,1,0:T(8,128)S(1)} %select_maximum_fusion.12, f32[4,26,16,1]{3,2,1,0:T(8,128)} %copy-done.14, ...), kind=kLoop, calls=%fused_computation.35 | loop fusion | flops 19267584 | bytes 14563072 | tf_op jit(solution)/shard_map/div | solution.py:110
  41.1 1.3 collective-permute-start.5
  42.4 1.3 collective-permute-start.6
  43.7 3.7 %collective-permute-done.6 = f32[4,1,16,256]{3,2,1,0:T(8,128)S(1)} collective-permute-done((f32[4,1,16,256]{3,2,1,0:T(8,128)S(1)}, f32[4,1,16,256]{3,2,1,0:T(8,128)S(1)}, u32[]{:S(2)}, u32[]{:S(2)}) %collective-permute-start.6) | collective-permute-done | bytes 65568 | tf_op jit(solution)/shard_map/ppermute | solution.py:36
  48.5 1.1 copy.74
  49.6 3.5 %collective-permute-start.7 = (f32[4,26,16,1]{1,2,3,0:T(8,128)}, f32[4,26,16,1]{1,2,3,0:T(8,128)S(1)}, u32[]{:S(2)}, u32[]{:S(2)}) collective-permute-start(f32[4,26,16,1]{1,2,3,0:T(8,128)} %copy.74), channel_id=1, source_target_pairs={{0,1},{1,2},{2,3},{3,4},{4,5},{5,6},{6,7},{7,8},{8,9},{9,10},{10,1... | collective-permute-start | bytes 19976 | tf_op jit(solution)/shard_map/ppermute | solution.py:33
  53.6 1.9 %collective-permute-start.8 = (f32[4,26,16,1]{1,2,3,0:T(8,128)S(1)}, f32[4,26,16,1]{1,2,3,0:T(8,128)}, u32[]{:S(2)}, u32[]{:S(2)}) collective-permute-start(f32[4,26,16,1]{1,2,3,0:T(8,128)S(1)} %copy.75), channel_id=1, source_target_pairs={{1,0},{2,1},{3,2},{4,3},{5,4},{6,5},{7,6},{8,7},{9,8},{10,9},{11,1... | collective-permute-start | bytes 19976 | tf_op jit(solution)/shard_map/ppermute | solution.py:36
  56.1 3.7 %collective-permute-done.8 = f32[4,26,16,1]{1,2,3,0:T(8,128)} collective-permute-done((f32[4,26,16,1]{1,2,3,0:T(8,128)S(1)}, f32[4,26,16,1]{1,2,3,0:T(8,128)}, u32[]{:S(2)}, u32[]{:S(2)}) %collective-permute-start.8) | collective-permute-done | bytes 6688 | tf_op jit(solution)/shard_map/ppermute | solution.py:36
  59.9 1.3 copy.54
  61.1 0.9 copy-done.18
  62.2 3.3 %select_maximum_fusion.8 = f32[4,26,18,258]{3,2,1,0:T(8,128)S(1)} fusion(f32[4,26,16,1]{3,2,1,0:T(8,128)S(1)} %copy.54, f32[4,26,16,1]{3,2,1,0:T(8,128)S(1)} %copy.53, f32[4,1,16,256]{3,2,1,0:T(8,128)} %copy-done.46, f32[4,24,16,256]{3,2,1,0:T(8,128)S(1)} %fusion.8, f32[4,1,16,256]{3,2,1,0:T(8,128)} %copy-done.43), kind=kLoop, calls=%fused_computation.11 | loop fusion | flops 5795712 | bytes 3649152 | tf_op jit(solution)/shard_map/concatenate | solution.py:37
  65.6 6.3 %fusion.56 = f32[4,24,16,256]{3,2,1,0:T(8,128)S(1)} fusion(f32[4,24,16,256]{3,2,1,0:T(8,128)S(1)} %fusion.8, f32[4,1,16,256]{3,2,1,0:T(8,128)S(1)} %copy-done.44, f32[4,1,16,256]{3,2,1,0:T(8,128)S(1)} %copy-done.47, f32[4,26,18,258]{3,2,1,0:T(8,128)S(1)} %select_maximum_fusion.8, f32[4,26,16,1]{3,2,1,0:T(8,128)} %copy-done.15, ...), kind=kLoop, calls=%fused_computation.108 | loop fusion | flops 21233664 | bytes 14563072 | tf_op jit(solution)/shard_map/add | solution.py:110
  71.9 1.3 collective-permute-start.10
  73.2 4.0 %collective-permute-start.9 = (f32[4,1,16,256]{3,2,1,0:T(8,128)S(1)}, f32[4,1,16,256]{3,2,1,0:T(8,128)S(1)}, u32[]{:S(2)}, u32[]{:S(2)}) collective-permute-start(f32[4,1,16,256]{3,2,1,0:T(8,128)S(1)} %get-tuple-element.39), channel_id=1, source_target_pairs={{0,16},{1,17},{2,18},{3,19},{4,20},{5,21},{6,22},{7,23},{8,24},{9,... | collective-permute-start | bytes 196616 | tf_op jit(solution)/shard_map/ppermute | solution.py:33
  77.2 1.3 collective-permute-done.9
  78.6 1.2 fusion.83
  79.8 1.7 %copy.76 = f32[4,26,16,1]{1,2,3,0:T(8,128)S(1)} copy(f32[4,26,16,1]{3,2,1,0:T(8,128)} %get-tuple-element.30) | data formatting | bytes 13312
  81.5 3.1 %collective-permute-start.11 = (f32[4,26,16,1]{1,2,3,0:T(8,128)S(1)}, f32[4,26,16,1]{1,2,3,0:T(8,128)S(1)}, u32[]{:S(2)}, u32[]{:S(2)}) collective-permute-start(f32[4,26,16,1]{1,2,3,0:T(8,128)S(1)} %copy.76), channel_id=1, source_target_pairs={{0,1},{1,2},{2,3},{3,4},{4,5},{5,6},{6,7},{7,8},{8,9},{9,10},{10,1... | collective-permute-start | bytes 19976 | tf_op jit(solution)/shard_map/ppermute | solution.py:33
  85.1 1.9 %collective-permute-start.12 = (f32[4,26,16,1]{1,2,3,0:T(8,128)S(1)}, f32[4,26,16,1]{1,2,3,0:T(8,128)S(1)}, u32[]{:S(2)}, u32[]{:S(2)}) collective-permute-start(f32[4,26,16,1]{1,2,3,0:T(8,128)S(1)} %copy.77), channel_id=1, source_target_pairs={{1,0},{2,1},{3,2},{4,3},{5,4},{6,5},{7,6},{8,7},{9,8},{10,9},{11,1... | collective-permute-start | bytes 19976 | tf_op jit(solution)/shard_map/ppermute | solution.py:36
  87.6 3.6 %collective-permute-done.12 = f32[4,26,16,1]{1,2,3,0:T(8,128)S(1)} collective-permute-done((f32[4,26,16,1]{1,2,3,0:T(8,128)S(1)}, f32[4,26,16,1]{1,2,3,0:T(8,128)S(1)}, u32[]{:S(2)}, u32[]{:S(2)}) %collective-permute-start.12) | collective-permute-done | bytes 6688 | tf_op jit(solution)/shard_map/ppermute | solution.py:36
  91.3 1.4 copy.60
  92.8 3.6 %select_maximum_fusion.4 = f32[4,26,18,258]{3,2,1,0:T(8,128)S(1)} fusion(f32[4,26,16,1]{3,2,1,0:T(8,128)} %copy.60, f32[4,26,16,1]{3,2,1,0:T(8,128)S(1)} %copy.59, f32[4,1,16,256]{3,2,1,0:T(8,128)S(1)} %collective-permute-done.10, f32[4,24,16,256]{3,2,1,0:T(8,128)S(1)} %fusion.56, f32[4,1,16,256]{3,2,1,0:T(8,128)S(1)} %collective-permute-done.9), kind=kLoop, calls=%fused_computation.7 | loop fusion | flops 5795712 | bytes 3649152 | tf_op jit(solution)/shard_map/concatenate | solution.py:37
  96.5 6.1 %fusion.37 = f32[4,24,16,256]{3,2,1,0:T(8,128)S(1)} fusion(f32[4,24,16,256]{3,2,1,0:T(8,128)S(1)} %fusion.56, f32[4,1,16,256]{3,2,1,0:T(8,128)} %copy-done.48, f32[4,1,16,256]{3,2,1,0:T(8,128)} %copy-done.45, f32[4,26,18,258]{3,2,1,0:T(8,128)S(1)} %select_maximum_fusion.4, f32[4,26,16,1]{3,2,1,0:T(8,128)} %copy-done.16, f32[4,26,16,1]{3,2,1,0:T(8,128)S(1)} %copy-done.19, ...), kind=kLoop, calls=%fused_computation.77 | loop fusion | flops 21233664 | bytes 14563072 | tf_op jit(solution)/shard_map/add | solution.py:110
  102.7 4.0 %collective-permute-start.13 = (f32[4,1,16,256]{3,2,1,0:T(8,128)S(1)}, f32[4,1,16,256]{3,2,1,0:T(8,128)S(1)}, u32[]{:S(2)}, u32[]{:S(2)}) collective-permute-start(f32[4,1,16,256]{3,2,1,0:T(8,128)S(1)} %get-tuple-element.37), channel_id=1, source_target_pairs={{0,16},{1,17},{2,18},{3,19},{4,20},{5,21},{6,22},{7,23},{8,24},{9,... | collective-permute-start | bytes 196616 | tf_op jit(solution)/shard_map/ppermute | solution.py:33
  106.7 1.3 collective-permute-start.14
  108.0 3.7 %collective-permute-done.14 = f32[4,1,16,256]{3,2,1,0:T(8,128)S(1)} collective-permute-done((f32[4,1,16,256]{3,2,1,0:T(8,128)S(1)}, f32[4,1,16,256]{3,2,1,0:T(8,128)S(1)}, u32[]{:S(2)}, u32[]{:S(2)}) %collective-permute-start.14) | collective-permute-done | bytes 65568 | tf_op jit(solution)/shard_map/ppermute | solution.py:36
  112.8 1.1 copy.78
  113.9 3.3 %collective-permute-start.15 = (f32[4,26,16,1]{1,2,3,0:T(8,128)}, f32[4,26,16,1]{1,2,3,0:T(8,128)S(1)}, u32[]{:S(2)}, u32[]{:S(2)}) collective-permute-start(f32[4,26,16,1]{1,2,3,0:T(8,128)} %copy.78), channel_id=1, source_target_pairs={{0,1},{1,2},{2,3},{3,4},{4,5},{5,6},{6,7},{7,8},{8,9},{9,10},{10,1... | collective-permute-start | bytes 19976 | tf_op jit(solution)/shard_map/ppermute | solution.py:33
  117.8 1.9 %collective-permute-start.16 = (f32[4,26,16,1]{1,2,3,0:T(8,128)S(1)}, f32[4,26,16,1]{1,2,3,0:T(8,128)}, u32[]{:S(2)}, u32[]{:S(2)}) collective-permute-start(f32[4,26,16,1]{1,2,3,0:T(8,128)S(1)} %copy.79), channel_id=1, source_target_pairs={{1,0},{2,1},{3,2},{4,3},{5,4},{6,5},{7,6},{8,7},{9,8},{10,9},{11,1... | collective-permute-start | bytes 19976 | tf_op jit(solution)/shard_map/ppermute | solution.py:36
  120.2 3.8 %collective-permute-done.16 = f32[4,26,16,1]{1,2,3,0:T(8,128)} collective-permute-done((f32[4,26,16,1]{1,2,3,0:T(8,128)S(1)}, f32[4,26,16,1]{1,2,3,0:T(8,128)}, u32[]{:S(2)}, u32[]{:S(2)}) %collective-permute-start.16) | collective-permute-done | bytes 6688 | tf_op jit(solution)/shard_map/ppermute | solution.py:36
  124.0 1.3 copy.66
  125.4 3.3 %select_maximum_fusion = f32[4,26,18,258]{3,2,1,0:T(8,128)S(1)} fusion(f32[4,26,16,1]{3,2,1,0:T(8,128)S(1)} %copy.66, f32[4,26,16,1]{3,2,1,0:T(8,128)S(1)} %copy.65, f32[4,1,16,256]{3,2,1,0:T(8,128)} %copy-done.41, f32[4,24,16,256]{3,2,1,0:T(8,128)S(1)} %fusion.37, f32[4,1,16,256]{3,2,1,0:T(8,128)} %copy-done.39), kind=kLoop, calls=%fused_computation.3 | loop fusion | flops 5795712 | bytes 3649152 | tf_op jit(solution)/shard_map/concatenate | solution.py:37
  128.8 5.9 %multiply_reduce_fusion = (f32[24,16,256]{2,1,0:T(8,128)S(1)}, f32[4,24,16,256]{3,2,1,0:T(8,128)}) fusion(f32[24]{0:T(128)S(1)} %get-tuple-element.51, f32[4,16,256]{2,1,0:T(8,128)S(1)} %copy-done.27, f32[24]{0:T(128)S(1)} %copy-done.56, f32[4,16,256]{2,1,0:T(8,128)S(1)} %copy-done.31, f32[24]{0:T(128)S(1)} %copy-done.60, f32[4,16,256]{2,1,0:T(8,128)S(1)} %copy-done.35, ...), kind=kLoop, calls=%fused_computation.149 | loop fusion | flops 21921792 | bytes 14956288 | tf_op jit(solution)/shard_map/reduce_sum | solution.py:132
  134.7 2.4 %fusion.89 = f32[24,16,256]{2,1,0:T(8,128)S(1)} fusion(f32[24,16,256]{2,1,0:T(8,128)S(1)} %get-tuple-element.21), kind=kOutput, calls=%fused_computation.183 | output fusion | flops 2260992 | bytes 786432 | tf_op jit(solution)/shard_map/jit(cumsum)/reduce_window_sum | solution.py:133
  137.1 3.3 %all_gather.3 = f32[2,16,256]{2,1,0:T(8,128)S(1)} all-gather(f32[1,16,256]{2,1,0:T(8,128)S(1)} %slice.336), channel_id=1, replica_groups=mesh['ply'=2,'tile'=16] {'ply'}, dimensions={0}, use_global_device_ids=true | all-gather | bytes 49152 | tf_op jit(solution)/shard_map/all_gather | solution.py:43
  (170 shorter events, 11.4 us)
Async XLA Ops:
  0.6 10.6 %copy-start = (f32[4,3,16,256]{3,2,1,0:T(8,128)S(1)}, f32[4,3,16,256]{3,2,1,0:T(8,128)}, u32[]{:S(2)}) copy-start(f32[4,3,16,256]{3,2,1,0:T(8,128)} %param.7) | copy-start | bytes 589828
  0.7 13.3 %collective-permute-start = (f32[4,1,16,256]{3,2,1,0:T(8,128)S(1)}, f32[4,1,16,256]{3,2,1,0:T(8,128)S(1)}, u32[]{:S(2)}, u32[]{:S(2)}) collective-permute-start(f32[4,1,16,256]{3,2,1,0:T(8,128)S(1)} %broadcast.119), channel_id=1, source_target_pairs={{0,16},{1,17},{2,18},{3,19},{4,20},{5,21},{6,22},{7,23},{8,24},{9,... | collective-permute-start | bytes 196616 | tf_op jit(solution)/shard_map/ppermute | solution.py:33
  3.9 10.1 %collective-permute-start.1 = (f32[4,1,16,256]{3,2,1,0:T(8,128)S(1)}, f32[4,1,16,256]{3,2,1,0:T(8,128)S(1)}, u32[]{:S(2)}, u32[]{:S(2)}) collective-permute-start(f32[4,1,16,256]{3,2,1,0:T(8,128)S(1)} %broadcast.119), channel_id=1, source_target_pairs={{16,0},{17,1},{18,2},{19,3},{20,4},{21,5},{22,6},{23,7},{24,8},{25... | collective-permute-start | bytes 196616 | tf_op jit(solution)/shard_map/ppermute | solution.py:36
  5.9 19.7 %collective-permute-start.4 = (f32[1,16,256]{2,1,0:T(8,128)S(1)}, f32[1,16,256]{2,1,0:T(8,128)S(1)}, u32[]{:S(2)}, u32[]{:S(2)}) collective-permute-start(f32[1,16,256]{2,1,0:T(8,128)S(1)} %slice.247), channel_id=1, source_target_pairs={{0,16},{1,17},{2,18},{3,19},{4,20},{5,21},{6,22},{7,23},{8,24},{9,... | collective-permute-start | bytes 49160 | tf_op jit(solution)/shard_map/ppermute | solution.py:25
  12.6 22.4 %copy-start.24 = (f32[4,16,256]{2,1,0:T(8,128)}, f32[4,16,256]{2,1,0:T(8,128)S(1)}, u32[]{:S(2)}) copy-start(f32[4,16,256]{2,1,0:T(8,128)S(1)} %get-tuple-element.46) | copy-start | bytes 196612
  12.6 22.4 %copy-start.28 = (f32[4,16,256]{2,1,0:T(8,128)}, f32[4,16,256]{2,1,0:T(8,128)S(1)}, u32[]{:S(2)}) copy-start(f32[4,16,256]{2,1,0:T(8,128)S(1)} %get-tuple-element.47) | copy-start | bytes 196612
  14.0 17.3 %copy-start.37 = (f32[4,1,16,256]{3,2,1,0:T(8,128)}, f32[4,1,16,256]{3,2,1,0:T(8,128)S(1)}, u32[]{:S(2)}) copy-start(f32[4,1,16,256]{3,2,1,0:T(8,128)S(1)} %collective-permute-done) | copy-start | bytes 196612
  14.0 17.3 %copy-start.38 = (f32[4,1,16,256]{3,2,1,0:T(8,128)}, f32[4,1,16,256]{3,2,1,0:T(8,128)S(1)}, u32[]{:S(2)}) copy-start(f32[4,1,16,256]{3,2,1,0:T(8,128)S(1)} %collective-permute-done.1) | copy-start | bytes 196612
  15.8 9.9 %copy-start.1 = (f32[24,16,256]{2,1,0:T(8,128)S(1)}, f32[24,16,256]{2,1,0:T(8,128)}, u32[]{:S(2)}) copy-start(f32[24,16,256]{2,1,0:T(8,128)} %param.11) | copy-start | bytes 1179652
  15.8 9.9 %slice-start = ((f32[24,16,256]{2,1,0:T(8,128)}), f32[23,16,256]{2,1,0:T(8,128)S(1)}, s32[]{:S(2)}) async-start(f32[24,16,256]{2,1,0:T(8,128)} %param.11), calls=%async_computation | async-start | bytes 753664 | tf_op jit(solution)/shard_map/slice | solution.py:126
  15.8 9.9 %copy-start.20 = (f32[24,16,256]{2,1,0:T(8,128)S(1)}, f32[24,16,256]{2,1,0:T(8,128)}, u32[]{:S(2)}) copy-start(f32[24,16,256]{2,1,0:T(8,128)} %param.10) | copy-start | bytes 1179652
  17.5 9.2 %collective-permute-start.2 = (f32[4,26,16,1]{1,2,3,0:T(8,128)S(1)}, f32[4,26,16,1]{1,2,3,0:T(8,128)S(1)}, u32[]{:S(2)}, u32[]{:S(2)}) collective-permute-start(f32[4,26,16,1]{1,2,3,0:T(8,128)S(1)} %copy.72), channel_id=1, source_target_pairs={{0,1},{1,2},{2,3},{3,4},{4,5},{5,6},{6,7},{7,8},{8,9},{9,10},{10,1... | collective-permute-start | bytes 19976 | tf_op jit(solution)/shard_map/ppermute | solution.py:33
  23.8 6.1 %collective-permute-start.3 = (f32[4,26,16,1]{1,2,3,0:T(8,128)S(1)}, f32[4,26,16,1]{1,2,3,0:T(8,128)S(1)}, u32[]{:S(2)}, u32[]{:S(2)}) collective-permute-start(f32[4,26,16,1]{1,2,3,0:T(8,128)S(1)} %copy.73), channel_id=1, source_target_pairs={{1,0},{2,1},{3,2},{4,3},{5,4},{6,5},{7,6},{8,7},{9,8},{10,9},{11,1... | collective-permute-start | bytes 19976 | tf_op jit(solution)/shard_map/ppermute | solution.py:36
  27.3 7.7 %copy-start.14 = (f32[4,26,16,1]{3,2,1,0:T(8,128)}, f32[4,26,16,1]{3,2,1,0:T(8,128)S(1)}, u32[]{:S(2)}) copy-start(f32[4,26,16,1]{3,2,1,0:T(8,128)S(1)} %copy.47) | copy-start | bytes 19972
  31.3 3.8 %copy-start.2 = (f32[24,16,256]{2,1,0:T(8,128)S(1)}, f32[24,16,256]{2,1,0:T(8,128)}, u32[]{:S(2)}) copy-start(f32[24,16,256]{2,1,0:T(8,128)} %param.11) | copy-start | bytes 1179652
  31.3 3.8 %copy-start.6 = (f32[24,16,256]{2,1,0:T(8,128)S(1)}, f32[24,16,256]{2,1,0:T(8,128)}, u32[]{:S(2)}) copy-start(f32[24,16,256]{2,1,0:T(8,128)} %get-tuple-element.42) | copy-start | bytes 1179652
  31.3 3.8 %copy-start.10 = (f32[24,16,256]{2,1,0:T(8,128)S(1)}, f32[24,16,256]{2,1,0:T(8,128)}, u32[]{:S(2)}) copy-start(f32[24,16,256]{2,1,0:T(8,128)} %get-tuple-element.43) | copy-start | bytes 1179652
  31.3 3.8 %copy-start.17 = (f32[4,26,16,1]{3,2,1,0:T(8,128)S(1)}, f32[4,26,16,1]{3,2,1,0:T(8,128)}, u32[]{:S(2)}) copy-start(f32[4,26,16,1]{3,2,1,0:T(8,128)} %copy.48) | copy-start | bytes 19972
  31.3 3.8 %copy-start.32 = (f32[4,16,256]{2,1,0:T(8,128)S(1)}, f32[4,16,256]{2,1,0:T(8,128)}, u32[]{:S(2)}) copy-start(f32[4,16,256]{2,1,0:T(8,128)} %get-tuple-element.48) | copy-start | bytes 196612
  31.3 3.8 %copy-start.36 = (f32[24,16,256]{2,1,0:T(8,128)S(1)}, f32[24,16,256]{2,1,0:T(8,128)}, u32[]{:S(2)}) copy-start(f32[24,16,256]{2,1,0:T(8,128)} %get-tuple-element.44) | copy-start | bytes 1179652
  31.3 3.8 %copy-start.49 = (f32[24]{0:T(128)S(1)}, f32[24]{0:T(128)}, u32[]{:S(2)}) copy-start(f32[24]{0:T(128)} %get-tuple-element.54) | copy-start | bytes 292
  31.3 3.8 %copy-start.53 = (f32[24]{0:T(128)S(1)}, f32[24]{0:T(128)}, u32[]{:S(2)}) copy-start(f32[24]{0:T(128)} %get-tuple-element.55) | copy-start | bytes 292
  31.3 3.8 %copy-start.57 = (f32[24]{0:T(128)S(1)}, f32[24]{0:T(128)}, u32[]{:S(2)}) copy-start(f32[24]{0:T(128)} %get-tuple-element.56) | copy-start | bytes 292
  31.4 3.8 %copy-start.61 = (f32[24]{0:T(128)S(1)}, f32[24]{0:T(128)}, u32[]{:S(2)}) copy-start(f32[24]{0:T(128)} %get-tuple-element.57) | copy-start | bytes 292
  41.1 2.6 %collective-permute-start.5 = (f32[4,1,16,256]{3,2,1,0:T(8,128)S(1)}, f32[4,1,16,256]{3,2,1,0:T(8,128)S(1)}, u32[]{:S(2)}, u32[]{:S(2)}) collective-permute-start(f32[4,1,16,256]{3,2,1,0:T(8,128)S(1)} %get-tuple-element.41), channel_id=1, source_target_pairs={{0,16},{1,17},{2,18},{3,19},{4,20},{5,21},{6,22},{7,23},{8,24},{9,... | collective-permute-start | bytes 196616 | tf_op jit(solution)/shard_map/ppermute | solution.py:33
  42.4 5.0 %collective-permute-start.6 = (f32[4,1,16,256]{3,2,1,0:T(8,128)S(1)}, f32[4,1,16,256]{3,2,1,0:T(8,128)S(1)}, u32[]{:S(2)}, u32[]{:S(2)}) collective-permute-start(f32[4,1,16,256]{3,2,1,0:T(8,128)S(1)} %get-tuple-element.40), channel_id=1, source_target_pairs={{16,0},{17,1},{18,2},{19,3},{20,4},{21,5},{22,6},{23,7},{24,8},{25... | collective-permute-start | bytes 196616 | tf_op jit(solution)/shard_map/ppermute | solution.py:36
  49.6 6.0 %collective-permute-start.7 = (f32[4,26,16,1]{1,2,3,0:T(8,128)}, f32[4,26,16,1]{1,2,3,0:T(8,128)S(1)}, u32[]{:S(2)}, u32[]{:S(2)}) collective-permute-start(f32[4,26,16,1]{1,2,3,0:T(8,128)} %copy.74), channel_id=1, source_target_pairs={{0,1},{1,2},{2,3},{3,4},{4,5},{5,6},{6,7},{7,8},{8,9},{9,10},{10,1... | collective-permute-start | bytes 19976 | tf_op jit(solution)/shard_map/ppermute | solution.py:33
  53.6 6.2 %collective-permute-start.8 = (f32[4,26,16,1]{1,2,3,0:T(8,128)S(1)}, f32[4,26,16,1]{1,2,3,0:T(8,128)}, u32[]{:S(2)}, u32[]{:S(2)}) collective-permute-start(f32[4,26,16,1]{1,2,3,0:T(8,128)S(1)} %copy.75), channel_id=1, source_target_pairs={{1,0},{2,1},{3,2},{4,3},{5,4},{6,5},{7,6},{8,7},{9,8},{10,9},{11,1... | collective-permute-start | bytes 19976 | tf_op jit(solution)/shard_map/ppermute | solution.py:36
  56.1 5.0 %copy-start.15 = (f32[4,26,16,1]{3,2,1,0:T(8,128)}, f32[4,26,16,1]{3,2,1,0:T(8,128)S(1)}, u32[]{:S(2)}) copy-start(f32[4,26,16,1]{3,2,1,0:T(8,128)S(1)} %copy.53) | copy-start | bytes 19972
  71.9 5.3 %collective-permute-start.10 = (f32[4,1,16,256]{3,2,1,0:T(8,128)S(1)}, f32[4,1,16,256]{3,2,1,0:T(8,128)S(1)}, u32[]{:S(2)}, u32[]{:S(2)}) collective-permute-start(f32[4,1,16,256]{3,2,1,0:T(8,128)S(1)} %get-tuple-element.38), channel_id=1, source_target_pairs={{16,0},{17,1},{18,2},{19,3},{20,4},{21,5},{22,6},{23,7},{24,8},{25... | collective-permute-start | bytes 196616 | tf_op jit(solution)/shard_map/ppermute | solution.py:36
  73.2 5.3 %collective-permute-start.9 = (f32[4,1,16,256]{3,2,1,0:T(8,128)S(1)}, f32[4,1,16,256]{3,2,1,0:T(8,128)S(1)}, u32[]{:S(2)}, u32[]{:S(2)}) collective-permute-start(f32[4,1,16,256]{3,2,1,0:T(8,128)S(1)} %get-tuple-element.39), channel_id=1, source_target_pairs={{0,16},{1,17},{2,18},{3,19},{4,20},{5,21},{6,22},{7,23},{8,24},{9,... | collective-permute-start | bytes 196616 | tf_op jit(solution)/shard_map/ppermute | solution.py:33
  77.2 15.4 %copy-start.45 = (f32[4,1,16,256]{3,2,1,0:T(8,128)}, f32[4,1,16,256]{3,2,1,0:T(8,128)S(1)}, u32[]{:S(2)}) copy-start(f32[4,1,16,256]{3,2,1,0:T(8,128)S(1)} %collective-permute-done.10) | copy-start | bytes 196612
  78.5 14.2 %copy-start.48 = (f32[4,1,16,256]{3,2,1,0:T(8,128)}, f32[4,1,16,256]{3,2,1,0:T(8,128)S(1)}, u32[]{:S(2)}) copy-start(f32[4,1,16,256]{3,2,1,0:T(8,128)S(1)} %collective-permute-done.9) | copy-start | bytes 196612
  81.5 5.6 %collective-permute-start.11 = (f32[4,26,16,1]{1,2,3,0:T(8,128)S(1)}, f32[4,26,16,1]{1,2,3,0:T(8,128)S(1)}, u32[]{:S(2)}, u32[]{:S(2)}) collective-permute-start(f32[4,26,16,1]{1,2,3,0:T(8,128)S(1)} %copy.76), channel_id=1, source_target_pairs={{0,1},{1,2},{2,3},{3,4},{4,5},{5,6},{6,7},{7,8},{8,9},{9,10},{10,1... | collective-permute-start | bytes 19976 | tf_op jit(solution)/shard_map/ppermute | solution.py:33
  85.1 6.1 %collective-permute-start.12 = (f32[4,26,16,1]{1,2,3,0:T(8,128)S(1)}, f32[4,26,16,1]{1,2,3,0:T(8,128)S(1)}, u32[]{:S(2)}, u32[]{:S(2)}) collective-permute-start(f32[4,26,16,1]{1,2,3,0:T(8,128)S(1)} %copy.77), channel_id=1, source_target_pairs={{1,0},{2,1},{3,2},{4,3},{5,4},{6,5},{7,6},{8,7},{9,8},{10,9},{11,1... | collective-permute-start | bytes 19976 | tf_op jit(solution)/shard_map/ppermute | solution.py:36
  87.6 5.1 %copy-start.16 = (f32[4,26,16,1]{3,2,1,0:T(8,128)}, f32[4,26,16,1]{3,2,1,0:T(8,128)S(1)}, u32[]{:S(2)}) copy-start(f32[4,26,16,1]{3,2,1,0:T(8,128)S(1)} %copy.59) | copy-start | bytes 19972
  92.7 3.8 %copy-start.4 = (f32[24,16,256]{2,1,0:T(8,128)S(1)}, f32[24,16,256]{2,1,0:T(8,128)}, u32[]{:S(2)}) copy-start(f32[24,16,256]{2,1,0:T(8,128)} %param.11) | copy-start | bytes 1179652
  92.7 3.8 %copy-start.8 = (f32[24,16,256]{2,1,0:T(8,128)S(1)}, f32[24,16,256]{2,1,0:T(8,128)}, u32[]{:S(2)}) copy-start(f32[24,16,256]{2,1,0:T(8,128)} %get-tuple-element.42) | copy-start | bytes 1179652
  92.7 3.8 %copy-start.12 = (f32[24,16,256]{2,1,0:T(8,128)S(1)}, f32[24,16,256]{2,1,0:T(8,128)}, u32[]{:S(2)}) copy-start(f32[24,16,256]{2,1,0:T(8,128)} %get-tuple-element.43) | copy-start | bytes 1179652
  92.7 3.8 %copy-start.19 = (f32[4,26,16,1]{3,2,1,0:T(8,128)S(1)}, f32[4,26,16,1]{3,2,1,0:T(8,128)}, u32[]{:S(2)}) copy-start(f32[4,26,16,1]{3,2,1,0:T(8,128)} %copy.60) | copy-start | bytes 19972
  92.7 3.8 %copy-start.22 = (f32[24,16,256]{2,1,0:T(8,128)S(1)}, f32[24,16,256]{2,1,0:T(8,128)}, u32[]{:S(2)}) copy-start(f32[24,16,256]{2,1,0:T(8,128)} %param.10) | copy-start | bytes 1179652
  92.7 3.7 %copy-start.26 = (f32[4,16,256]{2,1,0:T(8,128)S(1)}, f32[4,16,256]{2,1,0:T(8,128)}, u32[]{:S(2)}) copy-start(f32[4,16,256]{2,1,0:T(8,128)} %copy-done.24) | copy-start | bytes 196612
  92.7 3.7 %copy-start.30 = (f32[4,16,256]{2,1,0:T(8,128)S(1)}, f32[4,16,256]{2,1,0:T(8,128)}, u32[]{:S(2)}) copy-start(f32[4,16,256]{2,1,0:T(8,128)} %copy-done.28) | copy-start | bytes 196612
  92.7 3.7 %copy-start.34 = (f32[4,16,256]{2,1,0:T(8,128)S(1)}, f32[4,16,256]{2,1,0:T(8,128)}, u32[]{:S(2)}) copy-start(f32[4,16,256]{2,1,0:T(8,128)} %get-tuple-element.48) | copy-start | bytes 196612
  102.7 5.3 %collective-permute-start.13 = (f32[4,1,16,256]{3,2,1,0:T(8,128)S(1)}, f32[4,1,16,256]{3,2,1,0:T(8,128)S(1)}, u32[]{:S(2)}, u32[]{:S(2)}) collective-permute-start(f32[4,1,16,256]{3,2,1,0:T(8,128)S(1)} %get-tuple-element.37), channel_id=1, source_target_pairs={{0,16},{1,17},{2,18},{3,19},{4,20},{5,21},{6,22},{7,23},{8,24},{9,... | collective-permute-start | bytes 196616 | tf_op jit(solution)/shard_map/ppermute | solution.py:33
  106.7 5.0 %collective-permute-start.14 = (f32[4,1,16,256]{3,2,1,0:T(8,128)S(1)}, f32[4,1,16,256]{3,2,1,0:T(8,128)S(1)}, u32[]{:S(2)}, u32[]{:S(2)}) collective-permute-start(f32[4,1,16,256]{3,2,1,0:T(8,128)S(1)} %get-tuple-element.36), channel_id=1, source_target_pairs={{16,0},{17,1},{18,2},{19,3},{20,4},{21,5},{22,6},{23,7},{24,8},{25... | collective-permute-start | bytes 196616 | tf_op jit(solution)/shard_map/ppermute | solution.py:36
  113.9 5.8 %collective-permute-start.15 = (f32[4,26,16,1]{1,2,3,0:T(8,128)}, f32[4,26,16,1]{1,2,3,0:T(8,128)S(1)}, u32[]{:S(2)}, u32[]{:S(2)}) collective-permute-start(f32[4,26,16,1]{1,2,3,0:T(8,128)} %copy.78), channel_id=1, source_target_pairs={{0,1},{1,2},{2,3},{3,4},{4,5},{5,6},{6,7},{7,8},{8,9},{9,10},{10,1... | collective-permute-start | bytes 19976 | tf_op jit(solution)/shard_map/ppermute | solution.py:33
  117.8 6.2 %collective-permute-start.16 = (f32[4,26,16,1]{1,2,3,0:T(8,128)S(1)}, f32[4,26,16,1]{1,2,3,0:T(8,128)}, u32[]{:S(2)}, u32[]{:S(2)}) collective-permute-start(f32[4,26,16,1]{1,2,3,0:T(8,128)S(1)} %copy.79), channel_id=1, source_target_pairs={{1,0},{2,1},{3,2},{4,3},{5,4},{6,5},{7,6},{8,7},{9,8},{10,9},{11,1... | collective-permute-start | bytes 19976 | tf_op jit(solution)/shard_map/ppermute | solution.py:36
  (35 other events, 113.6 us)
where the time goes:
time: 142 us; the launch traced here: 141 us
  other arithmetic  46.3 us (33%)
  starting transfers between devices  43.8 us (31%)
  local copies, waits for them, and re-layouts  23.6 us (17%)
  waiting for transfers between devices  22.4 us (16%)
  blocking collectives  3.27 us (2%)
  between operations  1.85 us (1%)
    ppermute x8, starting transfers between devices, extended(): lax.ppermute(lax.slice_in_dim(block, block.shape[dim] - width, None, axis...  27 us
    ppermute x8, waiting for transfers between devices, extended(): lax.ppermute(lax.slice_in_dim(block, 0, width, axis=dim), axis, backward)  21.1 us
    concatenate x8, other arithmetic, extended(): block = jnp.concatenate([low, block, high], axis=dim)  14.3 us
    ppermute x8, starting transfers between devices, extended(): lax.ppermute(lax.slice_in_dim(block, 0, width, axis=dim), axis, backward)  12.8 us
    add x2, other arithmetic, sweep(): return centre + relaxation * (source - image) / diagonal_sum  12.4 us
    unnamed x138, local copies, waits for them, and re-layouts  11.3 us
    div x1, other arithmetic, sweep(): return centre + relaxation * (source - image) / diagonal_sum  5.93 us
    reduce_sum x1, other arithmetic, body(): summed = jnp.sum(adjoint * source, axis=0)  5.91 us
  transfers between devices with their start and end apart: 17, of which 7 were waited for; matrix products, arithmetic and copies ran while one was open for 10% of the time, Pallas kernels for 0%

commit v1 on v0

v1 whole, which is shorter than its diff:
```python
import functools

import jax
import jax.numpy as jnp
from jax import lax
from jax.experimental import pallas as pl
from jax.experimental.pallas import tpu as pltpu
from jax.sharding import PartitionSpec as P

HALO = 3
PAD = 4
LANES = 128
MESH = pl.DeviceIdType.MESH


def wide(row, rows, tiles):
    row = jnp.broadcast_to(row, (rows, LANES))
    return jnp.concatenate([row] * tiles, axis=1)


def kernel(
    groups,
    tiles,
    case_ref,
    angle_ref,
    strain_ref,
    stiff_hbm,
    inter_hbm,
    adjoint_ref,
    through_ref,
    stiff,
    inter,
    coef,
    strain,
    packed_out,
    packed_in,
    first,
    second,
    third,
    total_out,
    total_in,
    local_sem,
    pack_send,
    pack_recv,
    plane_send,
    plane_recv,
    total_send,
    total_recv,
):
    plies, rows, cols = inter_hbm.shape
    cases = strain_ref.shape[0]
    width = cols + LANES
    mine, tile = lax.axis_index("ply"), lax.axis_index("tile")

    def inside(dp, dt):
        p, t = mine + dp, tile + dt
        return (p >= 0) & (p < groups) & (t >= 0) & (t < tiles)

    has_below, has_above = inside(-1, 0), inside(1, 0)
    has_left, has_right = inside(0, -1), inside(0, 1)

    greeted = [(dp, dt) for dp in (-1, 0, 1) for dt in (-1, 0, 1) if (dp, dt) != (0, 0)]
    greeted += [(dp, 0) for dp in range(1 - groups, groups) if abs(dp) > 1]
    greeted = [(dp, dt) for dp, dt in greeted if abs(dp) < groups]

    locals_ = [
        pltpu.make_async_copy(
            inter_hbm, inter.at[pl.ds(PAD, plies), :, pl.ds(0, cols)], local_sem.at[0]
        ),
        pltpu.make_async_copy(
            stiff_hbm, stiff.at[pl.ds(PAD, plies), :, pl.ds(0, cols)], local_sem.at[1]
        ),
    ]
    for copy in locals_:
        copy.start()

    barrier = pltpu.get_barrier_semaphore()
    count = jnp.int32(0)
    for dp, dt in greeted:
        ok = inside(dp, dt)
        count = count + ok.astype(jnp.int32)

        @pl.when(ok)
        def _(dp=dp, dt=dt):
            pl.semaphore_signal(
                barrier, inc=1, device_id=(mine + dp, tile + dt), device_id_type=MESH
            )

    def table(p, carry):
        angle = angle_ref[p]
        cos_sq = jnp.where(angle == 0, 1.0, jnp.where(angle == 3, 0.0, 0.5))
        sin_sq = 1.0 - cos_sq
        mixed = jnp.where(angle == 1, 0.5, jnp.where(angle == 2, -0.5, 0.0))
        values = (
            4.0 * cos_sq + sin_sq,
            4.0 * sin_sq + cos_sq,
            1.5 * mixed,
            0.3 * cos_sq + 0.65 * sin_sq - 0.96 * mixed,
            0.3 * sin_sq + 0.65 * cos_sq + 0.96 * mixed,
            0.48 * (cos_sq - sin_sq) - 0.35 * mixed,
        )
        at = lax.broadcasted_iota(jnp.int32, (8, LANES), 0)
        block = jnp.zeros((8, LANES), jnp.float32)
        for k, value in enumerate(values):
            block = jnp.where(at == k, value, block)
        coef[p + PAD] = block
        return carry

    lax.fori_loop(0, plies, table, 0)

    def plane_copies(dp):
        if dp > 0:
            moves = [
                (inter_hbm.at[pl.ds(plies - PAD, PAD)], inter.at[pl.ds(0, PAD), :, pl.ds(0, cols)]),
                (stiff_hbm.at[pl.ds(plies - HALO, HALO)], stiff.at[pl.ds(1, HALO), :, pl.ds(0, cols)]),
                (coef.at[pl.ds(plies + 1, HALO)], coef.at[pl.ds(1, HALO)]),
            ]
        else:
            moves = [
                (inter_hbm.at[pl.ds(0, HALO)], inter.at[pl.ds(plies + PAD, HALO), :, pl.ds(0, cols)]),
                (stiff_hbm.at[pl.ds(0, HALO)], stiff.at[pl.ds(plies + PAD, HALO), :, pl.ds(0, cols)]),
                (coef.at[pl.ds(PAD, HALO)], coef.at[pl.ds(plies + PAD, HALO)]),
            ]
        side = int(dp > 0)
        return [
            pltpu.make_async_remote_copy(
                src_ref=src,
                dst_ref=dst,
                send_sem=plane_send.at[side, k],
                recv_sem=plane_recv.at[side, k],
                device_id=(mine + dp, tile),
                device_id_type=MESH,
            )
            for k, (src, dst) in enumerate(moves)
        ]

    pl.semaphore_wait(barrier, count)
    for dp in (1, -1):
        if groups > 1:

            @pl.when(inside(dp, 0))
            def _(dp=dp):
                for copy in plane_copies(dp):
                    copy.start()

    lane = lax.broadcasted_iota(jnp.int32, (rows, LANES), 1)
    slot = lane // 4
    low = jnp.zeros((rows, LANES), jnp.float32)
    high = jnp.zeros((rows, LANES), jnp.float32)
    for c in range(cases):
        for k in range(3):
            at = c * 3 + k
            plane = strain_ref[case_ref[c], k]
            strain[at, :, 0:cols] = plane
            head, tail = plane[:, :LANES], plane[:, cols - LANES :]
            low = jnp.where(slot == at, pltpu.roll(head, 4 * at, 1), low)
            high = jnp.where(slot == at, pltpu.roll(tail, 4 * at + 4, 1), high)
    packed_out[0, 2] = low
    packed_out[1, 2] = high

    for copy in locals_:
        copy.wait()

    def pack(p, carry):
        inter_low, inter_high, stiff_low, stiff_high = carry
        here = slot == p
        up, down = 4 * p, 4 * p + 4
        e = p + PAD
        inter_low = jnp.where(here, pltpu.roll(inter[e, :, 0:LANES], up, 1), inter_low)
        inter_high = jnp.where(here, pltpu.roll(inter[e, :, cols - LANES : cols], down, 1), inter_high)
        stiff_low = jnp.where(here, pltpu.roll(stiff[e, :, 0:LANES], up, 1), stiff_low)
        stiff_high = jnp.where(here, pltpu.roll(stiff[e, :, cols - LANES : cols], down, 1), stiff_high)
        return inter_low, inter_high, stiff_low, stiff_high

    zero = jnp.zeros((rows, LANES), jnp.float32)
    inter_low, inter_high, stiff_low, stiff_high = lax.fori_loop(0, plies, pack, (zero,) * 4)
    packed_out[0, 0] = inter_low
    packed_out[1, 0] = inter_high
    packed_out[0, 1] = stiff_low
    packed_out[1, 1] = stiff_high

    def pack_copy(dp, dt):
        depth = 3 if dp == 0 else 2
        group, side = 1 - dp, int(dt < 0)
        return pltpu.make_async_remote_copy(
            src_ref=packed_out.at[1 - side, pl.ds(0, depth)],
            dst_ref=packed_in.at[group, side, pl.ds(0, depth)],
            send_sem=pack_send.at[group, side],
            recv_sem=pack_recv.at[group, side],
            device_id=(mine + dp, tile + dt),
            device_id_type=MESH,
        )

    corners = [(dp, dt) for dp in (0, -1, 1) for dt in (-1, 1) if abs(dp) < groups]
    for dp, dt in corners:

        @pl.when(inside(dp, dt))
        def _(dp=dp, dt=dt):
            pack_copy(dp, dt).start()

    for group in range(3):
        for side, there in ((0, has_left), (1, has_right)):

            @pl.when(jnp.logical_not(there))
            def _(group=group, side=side):
                packed_in[group, side] = jnp.zeros((3, rows, LANES), jnp.float32)

    @pl.when(jnp.logical_not(has_below))
    def _():
        inter[PAD - 1] = jnp.zeros((rows, width), jnp.float32)
        for c in range(cases):
            for field in (first, second, third):
                field[c, PAD - 1] = jnp.zeros((rows, width), jnp.float32)

    @pl.when(jnp.logical_not(has_above))
    def _():
        for c in range(cases):
            for field in (first, second, third):
                field[c, plies + PAD] = jnp.zeros((rows, width), jnp.float32)

    for dp, dt in corners:

        @pl.when(inside(-dp, -dt))
        def _(dp=dp, dt=dt):
            pack_copy(dp, dt).wait_recv()

    for dp in (1, -1):
        if groups > 1:

            @pl.when(inside(-dp, 0))
            def _(dp=dp):
                for copy in plane_copies(dp):
                    copy.wait_recv()

    upper_half = lane < LANES // 2

    def halo_tile(group, kind, q):
        right = pltpu.roll(packed_in[group, 1, kind], lax.rem(LANES - 4 * q, LANES), 1)
        left = pltpu.roll(packed_in[group, 0, kind], LANES - 4 - 4 * q, 1)
        return jnp.where(upper_half, right, left)

    for at in range(3 * cases):
        strain[at, :, cols:width] = halo_tile(1, 2, jnp.int32(at))

    @pl.when(has_below)
    def _():
        inter[0, :, cols:width] = halo_tile(0, 0, jnp.int32(plies - PAD))

    reach = [
        (jnp.where(has_below, k, PAD), jnp.where(has_above, plies + 2 * PAD - k, plies + PAD))
        for k in (1, 2, 3)
    ]

    left_in = jnp.where(has_left, 2.0 / 3.0, 0.0)
    right_in = jnp.where(has_right, 2.0 / 3.0, 0.0)
    numerator = jnp.concatenate(
        [
            jnp.full((rows, cols), 2.0 / 3.0, jnp.float32),
            jnp.where(upper_half, right_in, left_in),
        ],
        axis=1,
    )

    def source_of(e, c, count):
        sx = strain[3 * c, :, 0 : count * LANES]
        sy = strain[3 * c + 1, :, 0 : count * LANES]
        sxy = strain[3 * c + 2, :, 0 : count * LANES]
        a, b, g = (wide(coef[e, k : k + 1, :], rows, count) for k in (3, 4, 5))
        return 1.1 + a * sx + b * sy + g * sxy

    def start(e, carry):
        group = (e + plies - PAD) // plies
        q = e - PAD - (group - 1) * plies
        inter[e, :, cols:width] = halo_tile(group, 0, q)
        rigid = jnp.concatenate([stiff[e, :, 0:cols], halo_tile(group, 1, q)], axis=1)
        weight = numerator / (10.0 + inter[e] + inter[e - 1] + rigid)
        stiff[e] = weight
        for c in range(cases):
            first[c, e] = weight * source_of(e, c, width // LANES)
        return carry

    lax.fori_loop(reach[0][0], reach[0][1], start, 0)

    row = lax.broadcasted_iota(jnp.int32, (rows, width), 0)
    not_top, not_bottom = row < rows - 1, row > 0

    def swept(e, c, field, tables):
        rows_c, cols_c, cross_c, weight, over, under = tables
        v = field[c, e]
        right = pltpu.roll(v, width - 1, 1)
        left = pltpu.roll(v, 1, 1)
        along = rows_c * v
        cross = cross_c * (right - left)
        upper = jnp.where(not_top, pltpu.roll(along + cross, rows - 1, 0), 0.0)
        lower = jnp.where(not_bottom, pltpu.roll(along - cross, 1, 0), 0.0)
        pull = (upper + lower) + cols_c * (right + left)
        pull = pull + (over * field[c, e + 1] + under * field[c, e - 1])
        return (v * (1.0 / 3.0) + first[c, e]) + weight * pull

    def tables_of(e):
        count = width // LANES
        rows_c, cols_c, cross_c = (wide(coef[e, k : k + 1, :], rows, count) for k in range(3))
        return rows_c, cols_c, cross_c, stiff[e], inter[e], inter[e - 1]

    for (begin, end), old, new in ((reach[1], first, second), (reach[2], second, third)):

        def step(e, carry, old=old, new=new):
            tables = tables_of(e)
            for c in range(cases):
                new[c, e] = swept(e, c, old, tables)
            return carry

        lax.fori_loop(begin, end, step, 0)

    share = 1.0 / (plies * groups)

    def last(p, running):
        e = p + PAD
        tables = tables_of(e)
        for c in range(cases):
            value = swept(e, c, third, tables)[:, 0:cols]
            adjoint_ref[c, p] = value
            running = running + value * source_of(e, c, cols // LANES)
        through_ref[p] = running * share
        return running

    running = lax.fori_loop(0, plies, last, jnp.zeros((rows, cols), jnp.float32))
    total_out[...] = running * share

    def total_copy(by):
        return pltpu.make_async_remote_copy(
            src_ref=total_out,
            dst_ref=total_in.at[by - 1],
            send_sem=total_send.at[by - 1],
            recv_sem=total_recv.at[by - 1],
            device_id=(mine + by, tile),
            device_id_type=MESH,
        )

    for by in range(1, groups):

        @pl.when(inside(by, 0))
        def _(by=by):
            total_copy(by).start()

    for dp, dt in corners:

        @pl.when(inside(dp, dt))
        def _(dp=dp, dt=dt):
            pack_copy(dp, dt).wait_send()

    for dp in (1, -1):
        if groups > 1:

            @pl.when(inside(dp, 0))
            def _(dp=dp):
                for copy in plane_copies(dp):
                    copy.wait_send()

    for by in range(1, groups):

        @pl.when(inside(-by, 0))
        def _(by=by):
            total_copy(by).wait_recv()

            def add(p, carry):
                through_ref[p] = through_ref[p] + total_in[by - 1]
                return carry

            lax.fori_loop(0, plies, add, 0)

    for by in range(1, groups):

        @pl.when(inside(by, 0))
        def _(by=by):
            total_copy(by).wait_send()


def body(groups, tiles, strain, case_ids, angle_ids, stiffening, interface):
    plies, rows, cols = interface.shape
    cases = strain.shape[0]
    ext, width = plies + 2 * PAD, cols + LANES
    vmem = lambda *shape: pltpu.VMEM(shape, jnp.float32)
    dma = pltpu.SemaphoreType.DMA
    others = max(groups - 1, 1)
    return pl.pallas_call(
        functools.partial(kernel, groups, tiles),
        out_shape=(
            jax.ShapeDtypeStruct((cases, plies, rows, cols), jnp.float32),
            jax.ShapeDtypeStruct((plies, rows, cols), jnp.float32),
        ),
        in_specs=[
            pl.BlockSpec(memory_space=pltpu.SMEM),
            pl.BlockSpec(memory_space=pltpu.SMEM),
            pl.BlockSpec(memory_space=pltpu.VMEM),
            pl.BlockSpec(memory_space=pl.ANY),
            pl.BlockSpec(memory_space=pl.ANY),
        ],
        out_specs=(
            pl.BlockSpec(memory_space=pltpu.VMEM),
            pl.BlockSpec(memory_space=pltpu.VMEM),
        ),
        scratch_shapes=[
            vmem(ext, rows, width),
            vmem(ext, rows, width),
            vmem(ext, 8, LANES),
            vmem(3 * cases, rows, width),
            vmem(2, 3, rows, LANES),
            vmem(3, 2, 3, rows, LANES),
            vmem(cases, ext, rows, width),
            vmem(cases, ext, rows, width),
            vmem(cases, ext, rows, width),
            vmem(rows, cols),
            vmem(others, rows, cols),
            dma((2,)),
            dma((3, 2)),
            dma((3, 2)),
            dma((2, 3)),
            dma((2, 3)),
            dma((others,)),
            dma((others,)),
        ],
        compiler_params=pltpu.CompilerParams(
            collective_id=0, has_side_effects=True, vmem_limit_bytes=40 * 1024 * 1024
        ),
    )(case_ids, angle_ids, strain, stiffening, interface)


def solution(mesh):
    return jax.shard_map(
        functools.partial(body, mesh.shape["ply"], mesh.shape["tile"]),
        mesh=mesh,
        in_specs=(
            P(None, None, None, "tile"),
            P(),
            P("ply"),
            P("ply", None, "tile"),
            P("ply", None, "tile"),
        ),
        out_specs=(P(None, "ply", None, "tile"), P("ply", None, "tile")),
        check_vma=False,
    )
```

time: 142 us -> 31.2 us (0.22)
  the two profiles are of different devices: /device:TPU:5 before, /device:TPU:10 now
where the time goes in v1:
time: 31.2 us; the launch traced here: 31 us
  Pallas kernels  24.2 us (78%)
  local copies, waits for them, and re-layouts  6.11 us (20%)
  between operations  0.65 us (2%)
    pallas_call x1, Pallas kernels, body(): pl.pallas_call(functools.partial(kernel, groups, tiles), out_shape=(jax.S...  24.2 us
    unnamed x12, local copies, waits for them, and re-layouts  6.11 us

profile of v1, /device:TPU:10, one launch (start us, length us, event | category | flops | bytes accessed | tf_op | source)
XLA Modules:
  0.0 31.0 jit_solution(210726850322923282)
XLA Ops:
  0.6 0.0 copy-start
  0.6 1.0 %copy-done = f32[24,16,256]{2,1,0:T(8,128)S(1)} copy-done((f32[24,16,256]{2,1,0:T(8,128)S(1)}, f32[24,16,256]{2,1,0:T(8,128)}, u32[]{:S(2)}) %copy-start) | copy-done | bytes 393240
  1.6 0.0 copy-start.1
  1.6 1.0 %copy-done.1 = f32[24,16,256]{2,1,0:T(8,128)S(1)} copy-done((f32[24,16,256]{2,1,0:T(8,128)S(1)}, f32[24,16,256]{2,1,0:T(8,128)}, u32[]{:S(2)}) %copy-start.1) | copy-done | bytes 393240
  2.6 0.0 copy-start.2
  2.6 0.9 %copy-done.2 = f32[4,3,16,256]{3,2,1,0:T(8,128)S(1)} copy-done((f32[4,3,16,256]{3,2,1,0:T(8,128)S(1)}, f32[4,3,16,256]{3,2,1,0:T(8,128)}, u32[]{:S(2)}) %copy-start.2) | copy-done | bytes 196632
  3.6 0.0 copy-start.3
  3.6 0.7 %copy-done.3 = s32[4]{0:T(128)S(1)} copy-done((s32[4]{0:T(128)S(1)}, s32[4]{0:T(128)}, u32[]{:S(2)}) %copy-start.3) | copy-done | bytes 40
  4.2 0.0 copy-start.4
  4.2 0.7 %copy-done.4 = s32[24]{0:T(128)S(1)} copy-done((s32[24]{0:T(128)S(1)}, s32[24]{0:T(128)}, u32[]{:S(2)}) %copy-start.4) | copy-done | bytes 120
  4.9 24.2 %shard_map.68 = (f32[4,24,16,256]{3,2,1,0:T(8,128)S(1)}, f32[24,16,256]{2,1,0:T(8,128)S(1)}) custom-call(s32[4]{0:T(128)S(1)} %copy-done.3, s32[24]{0:T(128)S(1)} %copy-done.4, f32[4,3,16,256]{3,2,1,0:T(8,128)S(1)} %copy-done.2, f32[24,16,256]{2,1,0:T(8,128)S(1)} %copy-done, f32[24,16,256]{2,1,0:T(8,128)S(1)} %copy-done.1), custom_call_target="tpu_custom_call" | custom-call | tf_op jit(solution)/shard_map/pallas_call | solution.py:386
  29.1 1.1 %copy.9 = f32[4,24,16,256]{3,2,1,0:T(8,128)} copy(f32[4,24,16,256]{3,2,1,0:T(8,128)S(1)} %get-tuple-element.4) | data formatting | bytes 3145728
  30.2 0.7 %copy.10 = f32[24,16,256]{2,1,0:T(8,128)} copy(f32[24,16,256]{2,1,0:T(8,128)S(1)} %get-tuple-element.5) | data formatting | bytes 786432
Async XLA Ops:
  0.6 1.0 %copy-start = (f32[24,16,256]{2,1,0:T(8,128)S(1)}, f32[24,16,256]{2,1,0:T(8,128)}, u32[]{:S(2)}) copy-start(f32[24,16,256]{2,1,0:T(8,128)} %stiff_hbm.1) | copy-start | bytes 1179652
  1.6 1.0 %copy-start.1 = (f32[24,16,256]{2,1,0:T(8,128)S(1)}, f32[24,16,256]{2,1,0:T(8,128)}, u32[]{:S(2)}) copy-start(f32[24,16,256]{2,1,0:T(8,128)} %inter_hbm.1) | copy-start | bytes 1179652
  2.6 0.9 %copy-start.2 = (f32[4,3,16,256]{3,2,1,0:T(8,128)S(1)}, f32[4,3,16,256]{3,2,1,0:T(8,128)}, u32[]{:S(2)}) copy-start(f32[4,3,16,256]{3,2,1,0:T(8,128)} %strain_ref.1) | copy-start | bytes 589828
  3.6 0.7 %copy-start.3 = (s32[4]{0:T(128)S(1)}, s32[4]{0:T(128)}, u32[]{:S(2)}) copy-start(s32[4]{0:T(128)} %case_ref.1) | copy-start | bytes 52
  4.2 0.7 %copy-start.4 = (s32[24]{0:T(128)S(1)}, s32[24]{0:T(128)}, u32[]{:S(2)}) copy-start(s32[24]{0:T(128)} %angle_ref.1) | copy-start | bytes 292

commit v2 on v1

--- a/solution.py
+++ b/solution.py
@@ -21,13 +21,16 @@
 def kernel(
     groups,
     tiles,
-    case_ref,
-    angle_ref,
-    strain_ref,
+    case_hbm,
+    angle_hbm,
+    strain_hbm,
     stiff_hbm,
     inter_hbm,
     adjoint_ref,
     through_ref,
+    case_ref,
+    angle_ref,
+    strain_ref,
     stiff,
     inter,
     coef,
@@ -48,7 +51,7 @@
     total_recv,
 ):
     plies, rows, cols = inter_hbm.shape
-    cases = strain_ref.shape[0]
+    cases = strain_hbm.shape[0]
     width = cols + LANES
     mine, tile = lax.axis_index("ply"), lax.axis_index("tile")
 
@@ -64,6 +67,9 @@
     greeted = [(dp, dt) for dp, dt in greeted if abs(dp) < groups]
 
     locals_ = [
+        pltpu.make_async_copy(angle_hbm, angle_ref, local_sem.at[2]),
+        pltpu.make_async_copy(case_hbm, case_ref, local_sem.at[3]),
+        pltpu.make_async_copy(strain_hbm, strain_ref, local_sem.at[4]),
         pltpu.make_async_copy(
             inter_hbm, inter.at[pl.ds(PAD, plies), :, pl.ds(0, cols)], local_sem.at[0]
         ),
@@ -85,6 +91,9 @@
             pl.semaphore_signal(
                 barrier, inc=1, device_id=(mine + dp, tile + dt), device_id_type=MESH
             )
+
+    for copy in locals_[:2]:
+        copy.wait()
 
     def table(p, carry):
         angle = angle_ref[p]
@@ -106,7 +115,7 @@
         coef[p + PAD] = block
         return carry
 
-    lax.fori_loop(0, plies, table, 0)
+    lax.fori_loop(0, plies, table, 0, unroll=4)
 
     def plane_copies(dp):
         if dp > 0:
@@ -145,6 +154,7 @@
 
     lane = lax.broadcasted_iota(jnp.int32, (rows, LANES), 1)
     slot = lane // 4
+    locals_[2].wait()
     low = jnp.zeros((rows, LANES), jnp.float32)
     high = jnp.zeros((rows, LANES), jnp.float32)
     for c in range(cases):
@@ -158,7 +168,7 @@
     packed_out[0, 2] = low
     packed_out[1, 2] = high
 
-    for copy in locals_:
+    for copy in locals_[3:]:
         copy.wait()
 
     def pack(p, carry):
@@ -173,7 +183,7 @@
         return inter_low, inter_high, stiff_low, stiff_high
 
     zero = jnp.zeros((rows, LANES), jnp.float32)
-    inter_low, inter_high, stiff_low, stiff_high = lax.fori_loop(0, plies, pack, (zero,) * 4)
+    inter_low, inter_high, stiff_low, stiff_high = lax.fori_loop(0, plies, pack, (zero,) * 4, unroll=8)
     packed_out[0, 0] = inter_low
     packed_out[1, 0] = inter_high
     packed_out[0, 1] = stiff_low
@@ -198,6 +208,27 @@
         def _(dp=dp, dt=dt):
             pack_copy(dp, dt).start()
 
+    def source_of(e, c, begin, count):
+        at = pl.ds(begin * LANES, count * LANES)
+        sx, sy, sxy = (strain[3 * c + k, :, at] for k in range(3))
+        a, b, g = (wide(coef[e, k : k + 1, :], rows, count) for k in (3, 4, 5))
+        return 1.1 + a * sx + b * sy + g * sxy
+
+    full = cols // LANES
+
+    def start_block(e):
+        rigid = inter[e, :, 0:cols] + inter[e - 1, :, 0:cols] + stiff[e, :, 0:cols]
+        weight = (2.0 / 3.0) / (10.0 + rigid)
+        stiff[e, :, 0:cols] = weight
+        for c in range(cases):
+            first[c, e, :, 0:cols] = weight * source_of(e, c, 0, full)
+
+    def start_own(e, carry):
+        start_block(e)
+        return carry
+
+    lax.fori_loop(PAD + 1, PAD + plies, start_own, 0, unroll=1)
+
     for group in range(3):
         for side, there in ((0, has_left), (1, has_right)):
 
@@ -242,47 +273,56 @@
     for at in range(3 * cases):
         strain[at, :, cols:width] = halo_tile(1, 2, jnp.int32(at))
 
+    start_block(PAD)
+
+    numerator = jnp.where(
+        upper_half, jnp.where(has_right, 2.0 / 3.0, 0.0), jnp.where(has_left, 2.0 / 3.0, 0.0)
+    )
+
+    def start_halo(e, group, q, under):
+        over = halo_tile(group, 0, q)
+        inter[e, :, cols:width] = over
+        weight = numerator / (10.0 + over + under + halo_tile(group, 1, q))
+        stiff[e, :, cols:width] = weight
+        for c in range(cases):
+            first[c, e, :, cols:width] = weight * source_of(e, c, full, 1)
+        return over
+
     @pl.when(has_below)
     def _():
-        inter[0, :, cols:width] = halo_tile(0, 0, jnp.int32(plies - PAD))
-
-    reach = [
-        (jnp.where(has_below, k, PAD), jnp.where(has_above, plies + 2 * PAD - k, plies + PAD))
-        for k in (1, 2, 3)
-    ]
-
-    left_in = jnp.where(has_left, 2.0 / 3.0, 0.0)
-    right_in = jnp.where(has_right, 2.0 / 3.0, 0.0)
-    numerator = jnp.concatenate(
-        [
-            jnp.full((rows, cols), 2.0 / 3.0, jnp.float32),
-            jnp.where(upper_half, right_in, left_in),
-        ],
-        axis=1,
+        under = halo_tile(0, 0, jnp.int32(plies - PAD))
+        inter[0, :, cols:width] = under
+
+        def below(e, under):
+            start_block(e)
+            return start_halo(e, 0, plies - PAD + e, under)
+
+        under = lax.fori_loop(1, PAD, below, under)
+
+    under = jnp.where(has_below, inter[PAD - 1, :, cols:width], 0.0)
+    under = lax.fori_loop(
+        0, plies, lambda p, under: start_halo(p + PAD, 1, p, under), under, unroll=4
     )
 
-    def source_of(e, c, count):
-        sx = strain[3 * c, :, 0 : count * LANES]
-        sy = strain[3 * c + 1, :, 0 : count * LANES]
-        sxy = strain[3 * c + 2, :, 0 : count * LANES]
-        a, b, g = (wide(coef[e, k : k + 1, :], rows, count) for k in (3, 4, 5))
-        return 1.1 + a * sx + b * sy + g * sxy
-
-    def start(e, carry):
-        group = (e + plies - PAD) // plies
-        q = e - PAD - (group - 1) * plies
-        inter[e, :, cols:width] = halo_tile(group, 0, q)
-        rigid = jnp.concatenate([stiff[e, :, 0:cols], halo_tile(group, 1, q)], axis=1)
-        weight = numerator / (10.0 + inter[e] + inter[e - 1] + rigid)
-        stiff[e] = weight
-        for c in range(cases):
-            first[c, e] = weight * source_of(e, c, width // LANES)
-        return carry
-
-    lax.fori_loop(reach[0][0], reach[0][1], start, 0)
-
-    row = lax.broadcasted_iota(jnp.int32, (rows, width), 0)
-    not_top, not_bottom = row < rows - 1, row > 0
+    @pl.when(has_above)
+    def _():
+        def above(q, under):
+            start_block(q + plies + PAD)
+            return start_halo(q + plies + PAD, 2, q, under)
+
+        lax.fori_loop(0, HALO, above, under)
+
+    half = rows // 2
+    row = lax.broadcasted_iota(jnp.int32, (half, width), 0)
+    is_last, is_first = row == half - 1, row == 0
+
+    def from_next_row(x):
+        a, b = (pltpu.roll(part, half - 1, 0) for part in (x[:half], x[half:]))
+        return jnp.concatenate([jnp.where(is_last, b, a), jnp.where(is_last, 0.0, b)], axis=0)
+
+    def from_row_before(x):
+        a, b = (pltpu.roll(part, 1, 0) for part in (x[:half], x[half:]))
+        return jnp.concatenate([jnp.where(is_first, 0.0, a), jnp.where(is_first, a, b)], axis=0)
 
     def swept(e, c, field, tables):
         rows_c, cols_c, cross_c, weight, over, under = tables
@@ -291,8 +331,8 @@
         left = pltpu.roll(v, 1, 1)
         along = rows_c * v
         cross = cross_c * (right - left)
-        upper = jnp.where(not_top, pltpu.roll(along + cross, rows - 1, 0), 0.0)
-        lower = jnp.where(not_bottom, pltpu.roll(along - cross, 1, 0), 0.0)
+        upper = from_next_row(along + cross)
+        lower = from_row_before(along - cross)
         pull = (upper + lower) + cols_c * (right + left)
         pull = pull + (over * field[c, e + 1] + under * field[c, e - 1])
         return (v * (1.0 / 3.0) + first[c, e]) + weight * pull
@@ -302,7 +342,7 @@
         rows_c, cols_c, cross_c = (wide(coef[e, k : k + 1, :], rows, count) for k in range(3))
         return rows_c, cols_c, cross_c, stiff[e], inter[e], inter[e - 1]
 
-    for (begin, end), old, new in ((reach[1], first, second), (reach[2], second, third)):
+    for depth, old, new in ((2, first, second), (1, second, third)):
 
         def step(e, carry, old=old, new=new):
             tables = tables_of(e)
@@ -310,7 +350,15 @@
                 new[c, e] = swept(e, c, old, tables)
             return carry
 
-        lax.fori_loop(begin, end, step, 0)
+        @pl.when(has_below)
+        def _(depth=depth, step=step):
+            lax.fori_loop(PAD - depth, PAD, step, 0)
+
+        @pl.when(has_above)
+        def _(depth=depth, step=step):
+            lax.fori_loop(plies + PAD, plies + PAD + depth, step, 0)
+
+        lax.fori_loop(PAD, plies + PAD, step, 0, unroll=2)
 
     share = 1.0 / (plies * groups)
 
@@ -320,11 +368,11 @@
         for c in range(cases):
             value = swept(e, c, third, tables)[:, 0:cols]
             adjoint_ref[c, p] = value
-            running = running + value * source_of(e, c, cols // LANES)
+            running = running + value * source_of(e, c, 0, full)
         through_ref[p] = running * share
         return running
 
-    running = lax.fori_loop(0, plies, last, jnp.zeros((rows, cols), jnp.float32))
+    running = lax.fori_loop(0, plies, last, jnp.zeros((rows, cols), jnp.float32), unroll=2)
     total_out[...] = running * share
 
     def total_copy(by):
@@ -367,7 +415,7 @@
                 through_ref[p] = through_ref[p] + total_in[by - 1]
                 return carry
 
-            lax.fori_loop(0, plies, add, 0)
+            lax.fori_loop(0, plies, add, 0, unroll=4)
 
     for by in range(1, groups):
 
@@ -389,18 +437,15 @@
             jax.ShapeDtypeStruct((cases, plies, rows, cols), jnp.float32),
             jax.ShapeDtypeStruct((plies, rows, cols), jnp.float32),
         ),
-        in_specs=[
-            pl.BlockSpec(memory_space=pltpu.SMEM),
-            pl.BlockSpec(memory_space=pltpu.SMEM),
-            pl.BlockSpec(memory_space=pltpu.VMEM),
-            pl.BlockSpec(memory_space=pl.ANY),
-            pl.BlockSpec(memory_space=pl.ANY),
-        ],
+        in_specs=[pl.BlockSpec(memory_space=pltpu.HBM)] * 5,
         out_specs=(
             pl.BlockSpec(memory_space=pltpu.VMEM),
             pl.BlockSpec(memory_space=pltpu.VMEM),
         ),
         scratch_shapes=[
+            pltpu.SMEM(case_ids.shape, jnp.int32),
+            pltpu.SMEM(angle_ids.shape, jnp.int32),
+            vmem(*strain.shape),
             vmem(ext, rows, width),
             vmem(ext, rows, width),
             vmem(ext, 8, LANES),
@@ -412,7 +457,7 @@
             vmem(cases, ext, rows, width),
             vmem(rows, cols),
             vmem(others, rows, cols),
-            dma((2,)),
+            dma((5,)),
             dma((3, 2)),
             dma((3, 2)),
             dma((2, 3)),

time: 31.2 us -> 25.5 us (0.82)
  the two profiles are of different devices: /device:TPU:10 before, /device:TPU:0 now
where the time goes in v2:
time: 25.5 us; the launch traced here: 25.2 us
  Pallas kernels  18.5 us (73%)
  local copies, waits for them, and re-layouts  6.11 us (24%)
  between operations  0.65 us (3%)
    pallas_call x1, Pallas kernels, body(): pl.pallas_call(functools.partial(kernel, groups, tiles), out_shape=(jax.S...  18.5 us
    unnamed x12, local copies, waits for them, and re-layouts  6.11 us

profile of v2, /device:TPU:0, one launch (start us, length us, event | category | flops | bytes accessed | tf_op | source)
XLA Modules:
  0.0 25.2 jit_solution(2398472910496435653)
XLA Ops:
  0.6 0.0 copy-start
  0.6 1.0 %copy-done = f32[24,16,256]{2,1,0:T(8,128)S(1)} copy-done((f32[24,16,256]{2,1,0:T(8,128)S(1)}, f32[24,16,256]{2,1,0:T(8,128)}, u32[]{:S(2)}) %copy-start) | copy-done | bytes 393240
  1.6 0.0 copy-start.1
  1.6 1.0 %copy-done.1 = f32[24,16,256]{2,1,0:T(8,128)S(1)} copy-done((f32[24,16,256]{2,1,0:T(8,128)S(1)}, f32[24,16,256]{2,1,0:T(8,128)}, u32[]{:S(2)}) %copy-start.1) | copy-done | bytes 393240
  2.6 0.0 copy-start.2
  2.6 0.9 %copy-done.2 = f32[4,3,16,256]{3,2,1,0:T(8,128)S(1)} copy-done((f32[4,3,16,256]{3,2,1,0:T(8,128)S(1)}, f32[4,3,16,256]{3,2,1,0:T(8,128)}, u32[]{:S(2)}) %copy-start.2) | copy-done | bytes 196632
  3.6 0.0 copy-start.3
  3.6 0.7 %copy-done.3 = s32[4]{0:T(128)S(1)} copy-done((s32[4]{0:T(128)S(1)}, s32[4]{0:T(128)}, u32[]{:S(2)}) %copy-start.3) | copy-done | bytes 40
  4.2 0.0 copy-start.4
  4.2 0.7 %copy-done.4 = s32[24]{0:T(128)S(1)} copy-done((s32[24]{0:T(128)S(1)}, s32[24]{0:T(128)}, u32[]{:S(2)}) %copy-start.4) | copy-done | bytes 120
  4.9 18.5 %shard_map.68 = (f32[4,24,16,256]{3,2,1,0:T(8,128)S(1)}, f32[24,16,256]{2,1,0:T(8,128)S(1)}) custom-call(s32[4]{0:T(128)S(1)} %copy-done.3, s32[24]{0:T(128)S(1)} %copy-done.4, f32[4,3,16,256]{3,2,1,0:T(8,128)S(1)} %copy-done.2, f32[24,16,256]{2,1,0:T(8,128)S(1)} %copy-done, f32[24,16,256]{2,1,0:T(8,128)S(1)} %copy-done.1), custom_call_target="tpu_custom_call" | custom-call | tf_op jit(solution)/shard_map/pallas_call | solution.py:434
  23.3 1.1 %copy.9 = f32[4,24,16,256]{3,2,1,0:T(8,128)} copy(f32[4,24,16,256]{3,2,1,0:T(8,128)S(1)} %get-tuple-element.4) | data formatting | bytes 3145728
  24.5 0.7 %copy.10 = f32[24,16,256]{2,1,0:T(8,128)} copy(f32[24,16,256]{2,1,0:T(8,128)S(1)} %get-tuple-element.5) | data formatting | bytes 786432
Async XLA Ops:
  0.6 1.0 %copy-start = (f32[24,16,256]{2,1,0:T(8,128)S(1)}, f32[24,16,256]{2,1,0:T(8,128)}, u32[]{:S(2)}) copy-start(f32[24,16,256]{2,1,0:T(8,128)} %stiff_hbm.1) | copy-start | bytes 1179652
  1.6 1.0 %copy-start.1 = (f32[24,16,256]{2,1,0:T(8,128)S(1)}, f32[24,16,256]{2,1,0:T(8,128)}, u32[]{:S(2)}) copy-start(f32[24,16,256]{2,1,0:T(8,128)} %inter_hbm.1) | copy-start | bytes 1179652
  2.6 0.9 %copy-start.2 = (f32[4,3,16,256]{3,2,1,0:T(8,128)S(1)}, f32[4,3,16,256]{3,2,1,0:T(8,128)}, u32[]{:S(2)}) copy-start(f32[4,3,16,256]{3,2,1,0:T(8,128)} %strain_hbm.1) | copy-start | bytes 589828
  3.6 0.7 %copy-start.3 = (s32[4]{0:T(128)S(1)}, s32[4]{0:T(128)}, u32[]{:S(2)}) copy-start(s32[4]{0:T(128)} %case_hbm.1) | copy-start | bytes 52
  4.2 0.7 %copy-start.4 = (s32[24]{0:T(128)S(1)}, s32[24]{0:T(128)}, u32[]{:S(2)}) copy-start(s32[24]{0:T(128)} %angle_hbm.1) | copy-start | bytes 292

commit v3 on v2

--- a/solution.py
+++ b/solution.py
@@ -26,7 +26,7 @@
     strain_hbm,
     stiff_hbm,
     inter_hbm,
-    adjoint_ref,
+    adjoint_hbm,
     through_ref,
     case_ref,
     angle_ref,
@@ -40,9 +40,11 @@
     first,
     second,
     third,
+    adjoint_ref,
     total_out,
     total_in,
     local_sem,
+    result_sem,
     pack_send,
     pack_recv,
     plane_send,
@@ -223,11 +225,14 @@
         for c in range(cases):
             first[c, e, :, 0:cols] = weight * source_of(e, c, 0, full)
 
-    def start_own(e, carry):
-        start_block(e)
+    def start_pair(i, carry):
+        for k in range(2):
+            start_block(PAD + 1 + 2 * i + k)
         return carry
 
-    lax.fori_loop(PAD + 1, PAD + plies, start_own, 0, unroll=1)
+    lax.fori_loop(0, (plies - 1) // 2, start_pair, 0)
+    if plies % 2 == 0:
+        start_block(PAD + plies - 1)
 
     for group in range(3):
         for side, there in ((0, has_left), (1, has_right)):
@@ -370,6 +375,9 @@
             adjoint_ref[c, p] = value
             running = running + value * source_of(e, c, 0, full)
         through_ref[p] = running * share
+        pltpu.make_async_copy(
+            adjoint_ref.at[:, pl.ds(p, 1)], adjoint_hbm.at[:, pl.ds(p, 1)], result_sem.at[0]
+        ).start()
         return running
 
     running = lax.fori_loop(0, plies, last, jnp.zeros((rows, cols), jnp.float32), unroll=2)
@@ -422,6 +430,8 @@
         @pl.when(inside(by, 0))
         def _(by=by):
             total_copy(by).wait_send()
+
+    pltpu.make_async_copy(adjoint_ref, adjoint_hbm, result_sem.at[0]).wait()
 
 
 def body(groups, tiles, strain, case_ids, angle_ids, stiffening, interface):
@@ -439,7 +449,7 @@
         ),
         in_specs=[pl.BlockSpec(memory_space=pltpu.HBM)] * 5,
         out_specs=(
-            pl.BlockSpec(memory_space=pltpu.VMEM),
+            pl.BlockSpec(memory_space=pltpu.HBM),
             pl.BlockSpec(memory_space=pltpu.VMEM),
         ),
         scratch_shapes=[
@@ -455,9 +465,11 @@
             vmem(cases, ext, rows, width),
             vmem(cases, ext, rows, width),
             vmem(cases, ext, rows, width),
+            vmem(cases, plies, rows, cols),
             vmem(rows, cols),
             vmem(others, rows, cols),
             dma((5,)),
+            dma((1,)),
             dma((3, 2)),
             dma((3, 2)),
             dma((2, 3)),
@@ -466,7 +478,7 @@
             dma((others,)),
         ],
         compiler_params=pltpu.CompilerParams(
-            collective_id=0, has_side_effects=True, vmem_limit_bytes=40 * 1024 * 1024
+            collective_id=0, has_side_effects=True, vmem_limit_bytes=56 * 1024 * 1024
         ),
     )(case_ids, angle_ids, strain, stiffening, interface)
 

time: 25.5 us -> 23.9 us (0.937)
  local copies, waits for them, and re-layouts: 6.11 us -> 3.47 us
  Pallas kernels: 18.5 us -> 19.6 us
    unnamed x12 -> x4, local copies, waits for them, and re-layouts: 6.11 us -> 3.47 us
    pallas_call x1, Pallas kernels: 18.5 us -> 19.6 us  [body(): pl.pallas_call(functools.partial(kernel, groups, tiles), out_shape=(jax.S...]
where the time goes in v3:
time: 23.9 us; the launch traced here: 23.7 us
  Pallas kernels  19.6 us (82%)
  local copies, waits for them, and re-layouts  3.47 us (15%)
  between operations  0.65 us (3%)
    pallas_call x1, Pallas kernels, body(): pl.pallas_call(functools.partial(kernel, groups, tiles), out_shape=(jax.S...  19.6 us
    unnamed x4, local copies, waits for them, and re-layouts  3.47 us

profile of v3, /device:TPU:0, one launch (start us, length us, event | category | flops | bytes accessed | tf_op | source)
XLA Modules:
  0.0 23.7 jit_solution(13948136128964024705)
XLA Ops:
  0.6 19.6 %shard_map.68 = (f32[4,24,16,256]{3,2,1,0:T(8,128)}, f32[24,16,256]{2,1,0:T(8,128)}) custom-call(s32[4]{0:T(128)} %case_hbm.1, s32[24]{0:T(128)} %angle_hbm.1, f32[4,3,16,256]{3,2,1,0:T(8,128)} %strain_hbm.1, f32[24,16,256]{2,1,0:T(8,128)} %stiff_hbm.1, f32[24,16,256]{2,1,0:T(8,128)} %inter_hbm.1), custom_call_target="tpu_custom_call" | custom-call | tf_op jit(solution)/shard_map/pallas_call | solution.py:444
  20.2 0.0 copy-start
  20.2 2.7 %copy.9 = f32[4,24,16,256]{3,2,1,0:T(8,128)} copy(f32[4,24,16,256]{3,2,1,0:T(8,128)} %get-tuple-element.4) | data formatting | bytes 3145728
  22.9 0.0 copy-done
  23.0 0.7 %copy.10 = f32[24,16,256]{2,1,0:T(8,128)} copy(f32[24,16,256]{2,1,0:T(8,128)S(1)} %copy-done) | data formatting | bytes 786432
Async XLA Ops:
  20.2 2.7 %copy-start = (f32[24,16,256]{2,1,0:T(8,128)S(1)}, f32[24,16,256]{2,1,0:T(8,128)}, u32[]{:S(2)}) copy-start(f32[24,16,256]{2,1,0:T(8,128)} %get-tuple-element.5) | copy-start | bytes 1179652

commit v4 on v3

--- a/solution.py
+++ b/solution.py
@@ -434,6 +434,35 @@
     pltpu.make_async_copy(adjoint_ref, adjoint_hbm, result_sem.at[0]).wait()
 
 
+def hand_over(parts, adjoint_in, through_in, adjoint_out, through_out, sem):
+    plies = through_in.shape[0]
+    step = plies // parts
+    copies = []
+    for k in range(parts):
+        at = pl.ds(k * step, step)
+        for c in range(adjoint_in.shape[0]):
+            copies.append((adjoint_in.at[c, at], adjoint_out.at[c, at]))
+        copies.append((through_in.at[at], through_out.at[at]))
+    copies = [pltpu.make_async_copy(a, b, sem.at[k]) for k, (a, b) in enumerate(copies)]
+    for copy in copies:
+        copy.start()
+    for copy in copies:
+        copy.wait()
+
+
+def handed_over(adjoint, through):
+    parts = 2 if through.shape[0] % 2 == 0 else 1
+    hbm = pl.BlockSpec(memory_space=pltpu.HBM)
+    return pl.pallas_call(
+        functools.partial(hand_over, parts),
+        out_shape=tuple(jax.ShapeDtypeStruct(a.shape, a.dtype) for a in (adjoint, through)),
+        in_specs=[hbm, hbm],
+        out_specs=(hbm, hbm),
+        scratch_shapes=[pltpu.SemaphoreType.DMA((parts * (adjoint.shape[0] + 1),))],
+        compiler_params=pltpu.CompilerParams(vmem_limit_bytes=56 * 1024 * 1024),
+    )(adjoint, through)
+
+
 def body(groups, tiles, strain, case_ids, angle_ids, stiffening, interface):
     plies, rows, cols = interface.shape
     cases = strain.shape[0]
@@ -441,7 +470,7 @@
     vmem = lambda *shape: pltpu.VMEM(shape, jnp.float32)
     dma = pltpu.SemaphoreType.DMA
     others = max(groups - 1, 1)
-    return pl.pallas_call(
+    adjoint, through = pl.pallas_call(
         functools.partial(kernel, groups, tiles),
         out_shape=(
             jax.ShapeDtypeStruct((cases, plies, rows, cols), jnp.float32),
@@ -481,6 +510,7 @@
             collective_id=0, has_side_effects=True, vmem_limit_bytes=56 * 1024 * 1024
         ),
     )(case_ids, angle_ids, strain, stiffening, interface)
+    return tuple(handed_over(adjoint, through))
 
 
 def solution(mesh):

time: 23.9 us -> 81.1 us (3.39)
  Pallas kernels: 19.6 us -> 80.3 us
  local copies, waits for them, and re-layouts: 3.47 us -> 0 us
    pallas_call x0 -> x1, Pallas kernels: none -> 60.8 us  [handed_over(): pl.pallas_call(functools.partial(hand_over, parts), out_shape=tuple((jax....]
    unnamed x4 -> x0, local copies, waits for them, and re-layouts: 3.47 us -> none
where the time goes in v4:
time: 81.1 us; the launch traced here: 81 us
  Pallas kernels  80.3 us (99%)
    pallas_call x1, Pallas kernels, handed_over(): pl.pallas_call(functools.partial(hand_over, parts), out_shape=tuple((jax....  60.8 us
    pallas_call x1, Pallas kernels, body(): pl.pallas_call(functools.partial(kernel, groups, tiles), out_shape=(jax.S...  19.6 us

profile of v4, /device:TPU:0, one launch (start us, length us, event | category | flops | bytes accessed | tf_op | source)
XLA Modules:
  0.0 81.0 jit_solution(5422898228686152684)
XLA Ops:
  0.6 19.6 %shard_map.68 = (f32[4,24,16,256]{3,2,1,0:T(8,128)}, f32[24,16,256]{2,1,0:T(8,128)}) custom-call(s32[4]{0:T(128)} %case_hbm.1, s32[24]{0:T(128)} %angle_hbm.1, f32[4,3,16,256]{3,2,1,0:T(8,128)} %strain_hbm.1, f32[24,16,256]{2,1,0:T(8,128)} %stiff_hbm.1, f32[24,16,256]{2,1,0:T(8,128)} %inter_hbm.1), custom_call_target="tpu_custom_call" | custom-call | tf_op jit(solution)/shard_map/pallas_call | solution.py:473
  20.2 60.8 %shard_map.69 = (f32[4,24,16,256]{3,2,1,0:T(8,128)}, f32[24,16,256]{2,1,0:T(8,128)}) custom-call(f32[4,24,16,256]{3,2,1,0:T(8,128)} %get-tuple-element.4.adjoint_in, f32[24,16,256]{2,1,0:T(8,128)} %get-tuple-element.5.through_in), custom_call_target="tpu_custom_call" | custom-call | tf_op jit(solution)/shard_map/pallas_call | solution.py:456

commit v5 on v4

--- a/solution.py
+++ b/solution.py
@@ -434,19 +434,23 @@
     pltpu.make_async_copy(adjoint_ref, adjoint_hbm, result_sem.at[0]).wait()
 
 
-def hand_over(parts, adjoint_in, through_in, adjoint_out, through_out, sem):
+def hand_over(parts, adjoint_in, through_in, adjoint_out, through_out, held, kept, sem, out_sem):
     plies = through_in.shape[0]
     step = plies // parts
     copies = []
     for k in range(parts):
         at = pl.ds(k * step, step)
         for c in range(adjoint_in.shape[0]):
-            copies.append((adjoint_in.at[c, at], adjoint_out.at[c, at]))
-        copies.append((through_in.at[at], through_out.at[at]))
-    copies = [pltpu.make_async_copy(a, b, sem.at[k]) for k, (a, b) in enumerate(copies)]
-    for copy in copies:
+            copies.append((adjoint_in.at[c, at], held.at[c, at], adjoint_out.at[c, at]))
+        copies.append((through_in.at[at], kept.at[at], through_out.at[at]))
+    inward = [pltpu.make_async_copy(a, b, sem.at[k]) for k, (a, b, _) in enumerate(copies)]
+    outward = [pltpu.make_async_copy(b, c, out_sem.at[k]) for k, (_, b, c) in enumerate(copies)]
+    for copy in inward:
         copy.start()
-    for copy in copies:
+    for arriving, leaving in zip(inward, outward):
+        arriving.wait()
+        leaving.start()
+    for copy in outward:
         copy.wait()
 
 
@@ -458,7 +462,12 @@
         out_shape=tuple(jax.ShapeDtypeStruct(a.shape, a.dtype) for a in (adjoint, through)),
         in_specs=[hbm, hbm],
         out_specs=(hbm, hbm),
-        scratch_shapes=[pltpu.SemaphoreType.DMA((parts * (adjoint.shape[0] + 1),))],
+        scratch_shapes=[
+            pltpu.VMEM(adjoint.shape, jnp.float32),
+            pltpu.VMEM(through.shape, jnp.float32),
+            pltpu.SemaphoreType.DMA((parts * (adjoint.shape[0] + 1),)),
+            pltpu.SemaphoreType.DMA((parts * (adjoint.shape[0] + 1),)),
+        ],
         compiler_params=pltpu.CompilerParams(vmem_limit_bytes=56 * 1024 * 1024),
     )(adjoint, through)
 

time: 81.1 us -> 22.8 us (0.28)
  Pallas kernels: 80.3 us -> 22 us
    pallas_call x1, Pallas kernels: 60.8 us -> 2.46 us  [handed_over(): pl.pallas_call(functools.partial(hand_over, parts), out_shape=tuple((jax....]
where the time goes in v5:
time: 22.8 us; the launch traced here: 22.7 us
  Pallas kernels  22 us (96%)
  between operations  0.64 us (3%)
    pallas_call x1, Pallas kernels, body(): pl.pallas_call(functools.partial(kernel, groups, tiles), out_shape=(jax.S...  19.6 us
    pallas_call x1, Pallas kernels, handed_over(): pl.pallas_call(functools.partial(hand_over, parts), out_shape=tuple((jax....  2.46 us

profile of v5, /device:TPU:0, one launch (start us, length us, event | category | flops | bytes accessed | tf_op | source)
XLA Modules:
  0.0 22.7 jit_solution(10880857530033750842)
XLA Ops:
  0.6 19.6 %shard_map.68 = (f32[4,24,16,256]{3,2,1,0:T(8,128)}, f32[24,16,256]{2,1,0:T(8,128)}) custom-call(s32[4]{0:T(128)} %case_hbm.1, s32[24]{0:T(128)} %angle_hbm.1, f32[4,3,16,256]{3,2,1,0:T(8,128)} %strain_hbm.1, f32[24,16,256]{2,1,0:T(8,128)} %stiff_hbm.1, f32[24,16,256]{2,1,0:T(8,128)} %inter_hbm.1), custom_call_target="tpu_custom_call" | custom-call | tf_op jit(solution)/shard_map/pallas_call | solution.py:482
  20.2 2.5 %shard_map.69 = (f32[4,24,16,256]{3,2,1,0:T(8,128)}, f32[24,16,256]{2,1,0:T(8,128)}) custom-call(f32[4,24,16,256]{3,2,1,0:T(8,128)} %get-tuple-element.4.adjoint_in, f32[24,16,256]{2,1,0:T(8,128)} %get-tuple-element.5.through_in), custom_call_target="tpu_custom_call" | custom-call | tf_op jit(solution)/shard_map/pallas_call | solution.py:460
